TPU v7x, 256 devices: a whole 4x4x8 slice. The times are simulated.
256 devices in a mesh: col: 64 (over y, z_lo, x, core), row: 4 (over z_hi).
Axes of the slice: x: 4, y: 4, z: 8 (z_hi: 4, z_lo: 2; z = z_hi * 2 + z_lo), core: 2. Of those that a mesh axis runs over, the one named last changes fastest.
Arguments:
- root_inverse: float32 [2048, 2048], P('row', 'col')
- child_inverse: float32 [256, 512, 512], P(('col', 'row'))
- child_panel: float32 [256, 1024, 512], P(('col', 'row')), may hold values from -0.375 to 0.375
- structure: int32 [256, 8], P(('col', 'row')), may hold values from 0 to 15, as said below
- widths: int32 [256], P(('col', 'row')), may hold values from 256 to 512
Outputs:
- sigma_root: float32 [2048, 2048], P('row', 'col')
- child_cross: float32 [256, 1024, 512], P(('col', 'row'))
- child_variance: float32 [256, 512], P(('col', 'row'))
Inputs may be any that keep to these rules, and one draw needn't show every extreme that they name: `structure`: each child names 8 distinct root blocks in rising order.
All inputs are finite; a program needn't handle non-finite values.
Results may differ from a plain program's by a relative error of at most 0.0003.
Values sent between devices are 32-bit elements; how exact they have to be, the bound alone decides.
No kernel may reach another device: no remote copies, remote signals or barrier semaphores. Data moves between devices by JAX's collectives and lax.ppermute only.
A program may use at most 192 MiB of HBM per device.

v0:
```python
import jax
import jax.numpy as jnp
from jax import lax
from jax.sharding import PartitionSpec as P

TILE = 128


def body(root_inverse, child_inverse, child_panel, structure, widths):
    partial_value = jnp.dot(
        lax.all_gather(root_inverse, "col", axis=1, tiled=True).T,
        root_inverse,
        precision=lax.Precision.HIGHEST,
        preferred_element_type=jnp.float32,
    )
    own_block = lax.psum_scatter(partial_value, "row", scatter_dimension=0, tiled=True)
    wide_rows = lax.all_gather(own_block, "col", axis=1, tiled=True)
    complete = lax.all_gather(wide_rows, "row", axis=0, tiled=True)
    tile_count = complete.shape[0] // TILE
    tiled = complete.reshape(tile_count, TILE, tile_count, TILE)

    def handle(items):
        inverse_block, panel_block, tiles, width_value = items
        column_ids = jnp.arange(inverse_block.shape[0], dtype=jnp.int32)
        live_cols = (column_ids < width_value).astype(jnp.float32)
        masked_inverse = inverse_block * live_cols[:, None] * live_cols[None, :]
        masked_panel = panel_block * live_cols[None, :]
        update = jnp.dot(
            masked_panel,
            masked_inverse,
            precision=lax.Precision.HIGHEST,
            preferred_element_type=jnp.float32,
        )
        picked = jnp.take(jnp.take(tiled, tiles, axis=0), tiles, axis=2)
        ancestor_block = picked.reshape(tiles.shape[0] * TILE, tiles.shape[0] * TILE)
        cross_block = -jnp.dot(
            ancestor_block,
            update,
            precision=lax.Precision.HIGHEST,
            preferred_element_type=jnp.float32,
        )
        variance = jnp.sum(masked_inverse * masked_inverse, axis=0) - jnp.sum(
            update * cross_block, axis=0
        )
        return (cross_block, variance)

    child_cross, child_variance = lax.map(handle, (child_inverse, child_panel, structure, widths))
    return (own_block, child_cross, child_variance)


def solution(mesh):
    placed = (
        P("row", "col"),
        P(("col", "row"), None, None),
        P(("col", "row"), None, None),
        P(("col", "row"), None),
        P(("col", "row")),
    )
    return jax.shard_map(
        body,
        mesh=mesh,
        in_specs=placed,
        out_specs=(P("row", "col"), P(("col", "row"), None, None), P(("col", "row"), None)),
        check_vma=False,
    )
```

profile of v0, /device:TPU:1, one launch (start us, length us, event | category | flops | bytes accessed | tf_op | source)
XLA Modules:
  0.0 641.0 jit_solution(5670676339828152946)
XLA Ops:
  7.2 0.0 all-gather.4.cloned.1.call-start
  7.2 0.7 all-gather.4.cloned.1.call-update
  7.9 0.0 reduce-scatter.2.cloned.1.call-start
  8.0 114.6 %all-gather.4.cloned.1.call-done = f32[512,2048]{0,1:T(8,128)} async-done(((f32[512,32]{0,1:T(8,128)}), f32[512,2048]{0,1:T(8,128)}) %all-gather.4.cloned.1.call-update) | async-done | bytes 4194320 | tf_op jit(solution)/shard_map/all_gather | solution.py:11
  122.5 6.8 %fusion.19 = f32[2048,32]{0,1:T(8,128)} fusion(f32[512,2048]{0,1:T(8,128)} %all-gather.4.cloned.1.call-done, f32[512,32]{0,1:T(8,128)} %param.5), kind=kOutput, calls=%fused_computation.32 | convolution fusion | flops 402653184 | bytes 4521984 | tf_op jit(solution)/shard_map/dot_general | solution.py:10
  129.3 0.0 reduce-scatter.2.cloned.1.call-update
  129.3 0.0 all-gather.6.cloned.1.call-start
  129.4 21.8 %reduce-scatter.2.cloned.1.call-done = f32[512,32]{0,1:T(8,128)} async-done(((f32[2048,32]{0,1:T(8,128)}), f32[512,32]{0,1:T(8,128)}) %reduce-scatter.2.cloned.1.call-update) | async-done | bytes 65552 | tf_op jit(solution)/shard_map/reduce_scatter | solution.py:16
  151.2 0.0 all-gather.6.cloned.1.call-update
  151.2 0.0 all-gather.8.cloned.1.call-start
  151.3 112.2 %all-gather.6.cloned.1.call-done = f32[512,2048]{0,1:T(8,128)} async-done(((f32[512,32]{0,1:T(8,128)}), f32[512,2048]{0,1:T(8,128)}) %all-gather.6.cloned.1.call-update) | async-done | bytes 4194320 | tf_op jit(solution)/shard_map/all_gather | solution.py:17
  264.2 0.2 fusion.9
  264.4 0.1 broadcast_bitcast_fusion
  264.5 5.2 fusion.2
  269.7 289.6 %all-gather.8.cloned.1.call-done = f32[2048,2048]{0,1:T(8,128)} async-done(((f32[512,2048]{0,1:T(8,128)}), f32[2048,2048]{0,1:T(8,128)}) %all-gather.8.cloned.1.call-update) | async-done | bytes 16777232 | tf_op jit(solution)/shard_map/all_gather | solution.py:18
  559.3 14.1 %copy.14 = f32[256,8,16,128]{3,2,1,0:T(8,128)} copy(f32[256,8,16,128]{3,1,2,0:T(8,128)} %bitcast.45) | data formatting | bytes 33554432
  573.4 21.5 %copy.11 = f32[16,128,16,128]{3,2,1,0:T(8,128)} copy(f32[16,128,16,128]{1,0,3,2:T(8,128)} %bitcast.43) | data formatting | bytes 33554432 | tf_op jit(solution)/shard_map/reshape | solution.py:20
  594.8 10.1 %gather_fusion = f32[8,128,16,128]{3,2,1,0:T(8,128)} fusion(f32[16,128,16,128]{3,2,1,0:T(8,128)} %copy.11, s32[1024]{0:T(1024)S(1)} %pad_clamp_fusion), kind=kCustom, calls=%fused_computation | custom fusion | bytes 16777248 | tf_op jit(solution)/shard_map/while/body/eval_jaxpr/jit(_take)/gather | solution.py:34
  604.9 4.2 broadcast_select_fusion
  609.1 5.7 copy.12
  614.8 6.2 gather_fusion.1
  621.0 4.6 copy.13
  625.5 8.3 %multiply_reduce_fusion = (f32[512]{0:T(512)S(1)}, f32[1,1024,512]{2,1,0:T(8,128)}) fusion(f32[1024,512]{1,0:T(8,128)S(1)} %fusion.2, f32[128,8,8,128]{3,2,1,0:T(8,128)S(1)} %bitcast.44, pred[1024]{0:T(1024)(128)(4,1)S(1)} %broadcast_bitcast_fusion), kind=kOutput, calls=%fused_computation.8 | convolution fusion | flops 6445071872 | bytes 8391680 | tf_op jit(solution)/shard_map/while/body/eval_jaxpr/dot_general | solution.py:36
  633.9 0.6 sub.14
  (9 shorter events, 0.0 us)
Async XLA Ops:
  7.2 115.4 %all-gather.4.cloned.1.call-start = ((), (), s32[]{:S(2)}) async-start(), calls=%async_computation.1 | async-start | bytes 4259840 | tf_op jit(solution)/shard_map/all_gather | solution.py:11
  7.9 256.3 %copy-start.1 = (s32[1,8]{1,0:T(1,128)S(1)}, s32[1,8]{1,0:T(1,128)}, u32[]{:S(2)}) copy-start(s32[1,8]{1,0:T(1,128)} %param.8) | copy-start | bytes 100
  7.9 256.3 %copy-start = (f32[1,512,512]{2,1,0:T(8,128)S(1)}, f32[1,512,512]{2,1,0:T(8,128)}, u32[]{:S(2)}) copy-start(f32[1,512,512]{2,1,0:T(8,128)} %param.6) | copy-start | bytes 3145732
  7.9 143.3 %reduce-scatter.2.cloned.1.call-start = ((), (), s32[]{:S(2)}) async-start(), calls=%async_computation.2 | async-start | bytes 327680 | tf_op jit(solution)/shard_map/reduce_scatter | solution.py:16
  129.3 134.1 %all-gather.6.cloned.1.call-start = ((), (), s32[]{:S(2)}) async-start(), calls=%async_computation.3 | async-start | bytes 4259840 | tf_op jit(solution)/shard_map/all_gather | solution.py:17
  151.2 408.0 %all-gather.8.cloned.1.call-start = ((), (), s32[]{:S(2)}) async-start(), calls=%async_computation.4 | async-start | bytes 20971520 | tf_op jit(solution)/shard_map/all_gather | solution.py:18
Sparse Core Ops, SparseCore 0:
  9.9 112.6 all-gather.3
  129.5 21.7 reduce-scatter.1
  153.8 109.6 all-gather.5
  265.3 293.9 all-gather.7
where the time goes:
time: 641 us
  waiting for transfers between devices  539 us (84%)
  local copies, waits for them, and re-layouts  62.2 us (10%)
  matrix products  20.3 us (3%)
  between operations  14.5 us (2%)
    all_gather x1, waiting for transfers between devices, body(): complete = lax.all_gather(wide_rows, 'row', axis=0, tiled=True)  290 us
    all_gather x1, waiting for transfers between devices, body(): lax.all_gather(root_inverse, 'col', axis=1, tiled=True)  115 us
    all_gather x1, waiting for transfers between devices, body(): wide_rows = lax.all_gather(own_block, 'col', axis=1, tiled=True)  112 us
    reduce_scatter x1, waiting for transfers between devices, body(): lax.psum_scatter(partial_value, 'row', scatter_dimension=0, tiled=True)  21.8 us
    reshape x1, local copies, waits for them, and re-layouts, body(): tiled = complete.reshape(tile_count, TILE, tile_count, TILE)  21.5 us
    gather x3, local copies, waits for them, and re-layouts, handle(): picked = jnp.take(jnp.take(tiled, tiles, axis=0), tiles, axis=2)  20.8 us
    unnamed x5, local copies, waits for them, and re-layouts  14.1 us
  transfers between devices with their start and end apart: 4, of which 4 were waited for; matrix products, arithmetic and copies ran while one was open for 1% of the time, Pallas kernels for 0%

commit v1 on v0

v1 whole, which is shorter than its diff:
```python
import itertools

import jax
import jax.numpy as jnp
from jax import lax
from jax.experimental import pallas as pl
from jax.experimental.pallas import tpu as pltpu
from jax.sharding import PartitionSpec as P

AXES = ("col", "row")
F32 = jnp.float32
BF16 = jnp.bfloat16
NN = (((1,), (0,)), ((), ()))
NT = (((1,), (1,)), ((), ()))


def flat(y, zl, x, c, zh):
    return (((y * 2 + zl) * 4 + x) * 2 + c) * 4 + zh


def places():
    return itertools.product(range(4), range(2), range(4), range(2), range(4))


def pairs(move):
    found = []
    for place in places():
        target = move(*place)
        if target is not None:
            found.append((flat(*place), flat(*target)))
    return found


def fold_move(y, zl, x, c, zh):
    target = {(0, 3): (3, 2), (0, 2): (3, 1), (1, 3): (2, 1)}.get((y, zh))
    return None if target is None else (target[0], zl, x, c, target[1])


def plane_move(step):
    return lambda y, zl, x, c, zh: (y, zl, x, c, (zh + step) % 4)


def pair_move(y, zl, x, c, zh):
    z = zh * 2 + zl
    near = z ^ 1 if c == 0 else (z + (1 if z % 2 else -1)) % 8
    return (y, near % 2, x, c, near // 2)


def first_move(step):
    def move(y, zl, x, c, zh):
        return ((y + step) % 4, zl, x, c, zh) if c == 0 else (y, zl, (x + step) % 4, c, zh)

    return move


def second_move(step):
    def move(y, zl, x, c, zh):
        return (y, zl, (x + step) % 4, c, zh) if c == 0 else ((y + step) % 4, zl, x, c, zh)

    return move


def core_move(y, zl, x, c, zh):
    return (y, zl, x, 1 - c, zh)


def send(value, move):
    return lax.ppermute(value, AXES, pairs(move))


def halves(value):
    high = value.astype(BF16)
    return high, (value - high.astype(F32)).astype(BF16)


def dot3(ah, al, bh, bl, dims):
    def one(a, b):
        return lax.dot_general(a, b, dims, preferred_element_type=F32)

    return one(ah, bh) + (one(ah, bl) + one(al, bh))


def update_kernel(width_ref, inverse_ref, panel_ref, high_ref, low_ref, square_ref):
    width = width_ref[0]
    inverse = inverse_ref[0]
    rows = lax.broadcasted_iota(jnp.int32, inverse.shape, 0)
    cols = lax.broadcasted_iota(jnp.int32, inverse.shape, 1)
    inverse = jnp.where((rows < width) & (cols < width), inverse, 0.0)
    square_ref[...] = jnp.sum(inverse * inverse, axis=0, keepdims=True)
    inverse_high, inverse_low = halves(inverse.T)
    for part in range(4):
        panel = panel_ref[0, pl.ds(part * 256, 256), :]
        live = lax.broadcasted_iota(jnp.int32, panel.shape, 1) < width
        panel_high, panel_low = halves(jnp.where(live, panel, 0.0))
        update = dot3(inverse_high, inverse_low, panel_high, panel_low, NT)
        high, low = halves(update)
        high_ref[:, pl.ds(part * 256, 256)] = high
        low_ref[:, pl.ds(part * 256, 256)] = low


def update(widths, child_inverse, child_panel):
    vmem = pl.BlockSpec(memory_space=pltpu.VMEM)
    return pl.pallas_call(
        update_kernel,
        out_shape=(
            jax.ShapeDtypeStruct((512, 1024), BF16),
            jax.ShapeDtypeStruct((512, 1024), BF16),
            jax.ShapeDtypeStruct((1, 512), F32),
        ),
        in_specs=[pl.BlockSpec(memory_space=pltpu.SMEM), vmem, vmem],
        out_specs=(vmem, vmem, vmem),
        compiler_params=pltpu.CompilerParams(vmem_limit_bytes=16 * 2**20),
        cost_estimate=pl.CostEstimate(flops=6 * 1024 * 512 * 512, bytes_accessed=5 * 2**20, transcendentals=0),
        name="update",
    )(widths, child_inverse, child_panel)


def final_kernel(
    where_ref, structure_ref, high_ref, low_ref, square_ref,
    q0, c10, c30, da0, db0, q1, c11, c31, da1, db1,
    cross_ref, variance_ref, sigma_ref,
    slot_ref, ah, al, sh, sl, oh, ol, th, tl, squares,
):
    y0, zl0, x0, core0, zh0 = (where_ref[i] for i in range(5))
    for block in range(16):
        slot_ref[block] = -1
    for t in range(8):
        slot_ref[structure_ref[0, t]] = t

    for t in range(8):
        superblock = structure_ref[0, t] // 4
        for r in range(3):
            @pl.when(superblock > r)
            def _():
                zero = jnp.zeros((128, 512), BF16)
                ah[pl.ds(t * 128, 128), pl.ds(r * 512, 512)] = zero
                al[pl.ds(t * 128, 128), pl.ds(r * 512, 512)] = zero
    for r in range(3):
        @pl.when(zh0 > r)
        def _():
            zero = jnp.zeros((512, 512), BF16)
            sh[:, pl.ds(r * 512, 512)] = zero
            sl[:, pl.ds(r * 512, 512)] = zero

        @pl.when(y0 > r)
        def _():
            zero = jnp.zeros((32, 512), BF16)
            oh[:, pl.ds(r * 512, 512)] = zero
            ol[:, pl.ds(r * 512, 512)] = zero

    def place(ref, count, base, d2, own):
        core = core0 if own else 1 - core0

        def step(i, carry):
            d1 = base + i // 2
            zr = i % 2
            y = jnp.where(core == 0, y0 - d1, y0 - d2) & 3
            x = jnp.where(core == 0, x0 - d2, x0 - d1) & 3
            zl = zl0 ^ zr
            inner = zl * 2 + x // 2
            part = (x & 1) * 2 + core
            mine = (zl == zl0) & (x == x0) & (core == core0)

            def segment(lane, size, group, k):
                slot = slot_ref[group * 4 + inner]

                def put(hi_ref, lo_ref, row):
                    high, low = halves(ref[i, :, pl.ds(lane, size)])
                    hi_ref[pl.ds(row, 32), pl.ds(k, size)] = high
                    lo_ref[pl.ds(row, 32), pl.ds(k, size)] = low

                @pl.when(slot >= 0)
                def _():
                    put(ah, al, pl.multiple_of(slot * 128 + part * 32, 32))

                @pl.when(zh0 == group)
                def _():
                    put(sh, sl, pl.multiple_of(inner * 128 + part * 32, 32))

                if own:
                    @pl.when(mine & (y0 == group))
                    def _():
                        put(oh, ol, 0)

            @pl.when(y == 0)
            def _():
                segment(0, 1280, 0, 0)

            @pl.when(y == 1)
            def _():
                segment(0, 1280, 1, 512)

            @pl.when(y == 2)
            def _():
                segment(0, 256, 1, 1792)
                segment(256, 1024, 2, 1024)

            @pl.when(y == 3)
            def _():
                segment(0, 768, 0, 1280)
                segment(768, 512, 3, 1536)

            return carry

        lax.fori_loop(0, count, step, 0)

    for own, (q, c1, c3, da, db) in ((True, (q0, c10, c30, da0, db0)), (False, (q1, c11, c31, da1, db1))):
        place(q, 8, 0, 0, own)
        place(c1, 8, 0, 1, own)
        place(c3, 8, 0, 3, own)
        place(da, 4, 0, 2, own)
        place(db, 4, 2, 2, own)

    squares[...] = jnp.zeros_like(squares)

    def times(r, carry):
        k = pl.multiple_of(r * 512, 512)
        live = jnp.int32(0)
        for q in range(4):
            live += (structure_ref[0, 2 * q] < 4 * (r + 1)).astype(jnp.int32)

        @pl.when(live == 0)
        def _():
            zero = jnp.zeros((512, 512), BF16)
            th[:, pl.ds(k, 512)] = zero
            tl[:, pl.ds(k, 512)] = zero

        for v in range(1, 5):
            @pl.when(live == v)
            def _():
                depth = 256 * v
                total = dot3(
                    high_ref[:, :depth], low_ref[:, :depth],
                    ah[:depth, pl.ds(k, 512)], al[:depth, pl.ds(k, 512)], NN,
                )
                high, low = halves(total)
                th[:, pl.ds(k, 512)] = high
                tl[:, pl.ds(k, 512)] = low
                square = total * total
                squares[...] += square[:, :128] + square[:, 128:256] + (square[:, 256:384] + square[:, 384:])

        return carry

    lax.fori_loop(0, 4, times, 0)

    def back(q, carry):
        row = pl.multiple_of(q * 256, 256)
        first = structure_ref[0, 2 * q] // 4
        for v in range(4):
            @pl.when(first == v)
            def _():
                k = 512 * v
                cross_ref[0, pl.ds(row, 256), :] = -dot3(
                    ah[pl.ds(row, 256), k:], al[pl.ds(row, 256), k:], th[:, k:], tl[:, k:], NT
                )

        return carry

    lax.fori_loop(0, 4, back, 0)
    variance_ref[...] = square_ref[...] + jnp.sum(squares[...].T, axis=0, keepdims=True)
    sigma_ref[...] = dot3(oh[...], ol[...], sh[...], sl[...], NT)


def final(where, structure, high, low, square, pieces):
    vmem = pl.BlockSpec(memory_space=pltpu.VMEM)
    smem = pl.BlockSpec(memory_space=pltpu.SMEM)
    return pl.pallas_call(
        final_kernel,
        out_shape=(
            jax.ShapeDtypeStruct((1, 1024, 512), F32),
            jax.ShapeDtypeStruct((1, 512), F32),
            jax.ShapeDtypeStruct((32, 512), F32),
        ),
        in_specs=[smem, smem] + [vmem] * 13,
        out_specs=(vmem, vmem, vmem),
        scratch_shapes=[
            pltpu.SMEM((16,), jnp.int32),
            pltpu.VMEM((1024, 2048), BF16), pltpu.VMEM((1024, 2048), BF16),
            pltpu.VMEM((512, 2048), BF16), pltpu.VMEM((512, 2048), BF16),
            pltpu.VMEM((32, 2048), BF16), pltpu.VMEM((32, 2048), BF16),
            pltpu.VMEM((512, 2048), BF16), pltpu.VMEM((512, 2048), BF16),
            pltpu.VMEM((512, 128), F32),
        ],
        compiler_params=pltpu.CompilerParams(vmem_limit_bytes=44 * 2**20),
        cost_estimate=pl.CostEstimate(flops=10**10, bytes_accessed=20 * 2**20, transcendentals=0),
        name="final",
    )(where, structure, high, low, square, *pieces)


def body(root_inverse, child_inverse, child_panel, structure, widths):
    col = lax.axis_index("col")
    zh0 = lax.axis_index("row")
    y0, zl0, x0, core0 = col // 16, (col // 8) % 2, (col // 2) % 4, col % 2
    where = jnp.stack([y0, zl0, x0, core0, zh0]).astype(jnp.int32)
    high, low, square = update(widths, child_inverse, child_panel)

    own = root_inverse.T
    folded = send(own, fold_move)
    moved = ((y0 == 3) & ((zh0 == 1) | (zh0 == 2))) | ((y0 == 2) & (zh0 == 1))
    own = jnp.where(moved, folded, own)
    planes = jnp.stack([own, send(own, plane_move(1)), send(own, plane_move(2)), send(own, plane_move(3))])
    base = jnp.where(y0 == 0, 0, 1)
    wide = jnp.concatenate([planes[(zh0 - base - s) % 4] for s in range(3)], axis=1)
    line = lax.dynamic_slice(wide, (0, jnp.where(y0 >= 2, 256, 0)), (32, 1280))
    both = jnp.stack([line, send(line, pair_move)])
    quad = jnp.concatenate(
        [both, send(both, first_move(1)), send(both, first_move(2)), send(both, first_move(3))], axis=0
    )
    from_left = send(quad, second_move(1))
    from_right = send(quad, second_move(3))
    far_a = send(from_left[:4], second_move(1))
    far_b = send(from_right[4:], second_move(3))
    mine = [quad, from_left, from_right, far_a, far_b]
    others = [send(piece, core_move) for piece in mine]
    cross, variance, sigma = final(where, structure, high, low, square, mine + others)
    return sigma.T, cross, variance


def solution(mesh):
    placed = (
        P("row", "col"),
        P(("col", "row"), None, None),
        P(("col", "row"), None, None),
        P(("col", "row"), None),
        P(("col", "row")),
    )
    return jax.shard_map(
        body,
        mesh=mesh,
        in_specs=placed,
        out_specs=(P("row", "col"), P(("col", "row"), None, None), P(("col", "row"), None)),
        check_vma=False,
    )
```

time: 641 us -> 113 us (0.18)
  waiting for transfers between devices: 539 us -> 30.6 us
  local copies, waits for them, and re-layouts: 62.2 us -> 5.94 us
  starting transfers between devices: 0.16 us -> 50.2 us
  Pallas kernels: 0 us -> 23.2 us
  matrix products: 20.3 us -> 0 us
  between operations: 14.5 us -> 1.45 us
    all_gather x3 -> x0, waiting for transfers between devices: 516 us -> none  [the longest x1 290 us: body(): complete = lax.all_gather(wide_rows, 'row', axis=0, tiled=True)]
    ppermute x0 -> x17, starting transfers between devices: none -> 50.2 us  [send(): return lax.ppermute(value, AXES, pairs(move))]
    ppermute x0 -> x17, waiting for transfers between devices: none -> 30.6 us  [send(): return lax.ppermute(value, AXES, pairs(move))]
    pallas_call x0 -> x2, Pallas kernels: none -> 23.2 us  [the longest x1 21.3 us: final(): pl.pallas_call(final_kernel, out_shape=(jax.ShapeDtypeStruct((1, 1024, 51...]
    reduce_scatter x1 -> x0, waiting for transfers between devices: 21.8 us -> none  [body(): lax.psum_scatter(partial_value, 'row', scatter_dimension=0, tiled=True)]
    reshape x1 -> x0, local copies, waits for them, and re-layouts: 21.5 us -> none  [body(): tiled = complete.reshape(tile_count, TILE, tile_count, TILE)]
    gather x3 -> x0, local copies, waits for them, and re-layouts: 20.8 us -> none  [handle(): picked = jnp.take(jnp.take(tiled, tiles, axis=0), tiles, axis=2)]
    dot_general x3 -> x0, matrix products: 20.3 us -> none  [the longest x1 8.34 us: handle(): jnp.dot(ancestor_block, update, precision=lax.Precision.HIGHEST, preferre...]
  transfers between devices with their start and end apart: 4 -> 17, of which waited for: 4 -> 5; matrix products, arithmetic and copies ran while one was open for 1% -> 2% of each run, Pallas kernels for 0% -> 2%
where the time goes in v1:
time: 113 us
  starting transfers between devices  50.2 us (44%)
  waiting for transfers between devices  30.6 us (27%)
  Pallas kernels  23.2 us (21%)
  local copies, waits for them, and re-layouts  5.94 us (5%)
  other arithmetic  1.59 us (1%)
  between operations  1.45 us (1%)
    ppermute x17, starting transfers between devices, send(): return lax.ppermute(value, AXES, pairs(move))  50.2 us
    ppermute x17, waiting for transfers between devices, send(): return lax.ppermute(value, AXES, pairs(move))  30.6 us
    pallas_call x1, Pallas kernels, final(): pl.pallas_call(final_kernel, out_shape=(jax.ShapeDtypeStruct((1, 1024, 51...  21.3 us
    unnamed x9, local copies, waits for them, and re-layouts  5 us
  transfers between devices with their start and end apart: 17, of which 5 were waited for; matrix products, arithmetic and copies ran while one was open for 2% of the time, Pallas kernels for 2%

profile of v1, /device:TPU:1, one launch (start us, length us, event | category | flops | bytes accessed | tf_op | source)
XLA Modules:
  0.0 113.0 jit_solution(3731902670244126574)
XLA Ops:
  1.3 0.9 broadcast_select_fusion
  2.2 13.4 %collective-permute-start.3 = (f32[32,512]{1,0:T(8,128)S(1)}, f32[32,512]{1,0:T(8,128)S(1)}, u32[]{:S(2)}, u32[]{:S(2)}) collective-permute-start(f32[32,512]{1,0:T(8,128)S(1)} %broadcast_select_fusion), channel_id=1, source_target_pairs={{0,3},{1,0},{2,1},{3,2},{4,7},{5,4},{6,5},{7,6},{8,11},{9,8},{10,9... | collective-permute-start | bytes 196616 | tf_op jit(solution)/shard_map/ppermute | solution.py:68
  15.6 2.2 %collective-permute-start.1 = (f32[32,512]{1,0:T(8,128)S(1)}, f32[32,512]{1,0:T(8,128)S(1)}, u32[]{:S(2)}, u32[]{:S(2)}) collective-permute-start(f32[32,512]{1,0:T(8,128)S(1)} %broadcast_select_fusion), channel_id=1, source_target_pairs={{0,1},{1,2},{2,3},{3,0},{4,5},{5,6},{6,7},{7,4},{8,9},{9,10},{10,1... | collective-permute-start | bytes 196616 | tf_op jit(solution)/shard_map/ppermute | solution.py:68
  17.8 5.3 %collective-permute-done.2 = f32[32,512]{1,0:T(8,128)S(1)} collective-permute-done((f32[32,512]{1,0:T(8,128)S(1)}, f32[32,512]{1,0:T(8,128)S(1)}, u32[]{:S(2)}, u32[]{:S(2)}) %collective-permute-start.2) | collective-permute-done | bytes 65568 | tf_op jit(solution)/shard_map/ppermute | solution.py:68
  23.1 0.7 constant_dynamic-update-slice_fusion.4
  23.8 2.0 %collective-permute-start.4 = (f32[32,1280]{1,0:T(8,128)S(1)}, f32[32,1280]{1,0:T(8,128)S(1)}, u32[]{:S(2)}, u32[]{:S(2)}) collective-permute-start(f32[32,1280]{1,0:T(8,128)S(1)} %get-tuple-element.16), channel_id=1, source_target_pairs={{0,32},{1,33},{2,34},{3,35},{4,39},{5,36},{6,37},{7,38},{8,40},{9,... | collective-permute-start | bytes 491528 | tf_op jit(solution)/shard_map/ppermute | solution.py:68
  25.9 3.3 %collective-permute-done.4 = f32[32,1280]{1,0:T(8,128)S(1)} collective-permute-done((f32[32,1280]{1,0:T(8,128)S(1)}, f32[32,1280]{1,0:T(8,128)S(1)}, u32[]{:S(2)}, u32[]{:S(2)}) %collective-permute-start.4) | collective-permute-done | bytes 163872 | tf_op jit(solution)/shard_map/ppermute | solution.py:68
  29.2 2.6 %collective-permute-start.7 = (f32[2,32,1280]{2,1,0:T(8,128)S(1)}, f32[2,32,1280]{2,1,0:T(8,128)S(1)}, u32[]{:S(2)}, u32[]{:S(2)}) collective-permute-start(f32[2,32,1280]{2,1,0:T(8,128)S(1)} %pad_maximum_fusion), channel_id=1, source_target_pairs={{0,192},{1,193},{2,194},{3,195},{4,28},{5,29},{6,30},{7,31},{8,200... | collective-permute-start | bytes 983048 | tf_op jit(solution)/shard_map/ppermute | solution.py:68
  33.6 9.4 %collective-permute-done.5 = f32[2,32,1280]{2,1,0:T(8,128)S(1)} collective-permute-done((f32[2,32,1280]{2,1,0:T(8,128)S(1)}, f32[2,32,1280]{2,1,0:T(8,128)S(1)}, u32[]{:S(2)}, u32[]{:S(2)}) %collective-permute-start.5) | collective-permute-done | bytes 327712 | tf_op jit(solution)/shard_map/ppermute | solution.py:68
  43.0 0.8 constant_dynamic-update-slice_fusion.2
  43.8 0.8 constant_dynamic-update-slice_fusion.1
  44.5 0.7 constant_dynamic-update-slice_fusion.q0
  45.3 5.3 %collective-permute-start.9 = (f32[8,32,1280]{2,1,0:T(8,128)}, f32[8,32,1280]{2,1,0:T(8,128)S(1)}, u32[]{:S(2)}, u32[]{:S(2)}) collective-permute-start(f32[8,32,1280]{2,1,0:T(8,128)} %constant_dynamic-update-slice_fusion.q0), channel_id=1, source_target_pairs={{0,24},{1,25},{2,26},{3,27},{4,196},{5,197},{6,198},{7,199},{8,0},... | collective-permute-start | bytes 3932168 | tf_op jit(solution)/shard_map/ppermute | solution.py:68
  50.6 4.3 %collective-permute-start.12 = (f32[8,32,1280]{2,1,0:T(8,128)}, f32[8,32,1280]{2,1,0:T(8,128)}, u32[]{:S(2)}, u32[]{:S(2)}) collective-permute-start(f32[8,32,1280]{2,1,0:T(8,128)} %constant_dynamic-update-slice_fusion.q0), channel_id=1, source_target_pairs={{0,4},{1,5},{2,6},{3,7},{4,0},{5,1},{6,2},{7,3},{8,12},{9,13},{10,... | collective-permute-start | bytes 3932168 | tf_op jit(solution)/shard_map/ppermute | solution.py:68
  54.9 10.5 %collective-permute-done.9.c30 = f32[8,32,1280]{2,1,0:T(8,128)S(1)} collective-permute-done((f32[8,32,1280]{2,1,0:T(8,128)}, f32[8,32,1280]{2,1,0:T(8,128)S(1)}, u32[]{:S(2)}, u32[]{:S(2)}) %collective-permute-start.9) | collective-permute-done | bytes 1310752 | tf_op jit(solution)/shard_map/ppermute | solution.py:68
  65.5 3.4 %collective-permute-start.11 = (f32[4,32,1280]{2,1,0:T(8,128)S(1)}, f32[4,32,1280]{2,1,0:T(8,128)S(1)}, u32[]{:S(2)}, u32[]{:S(2)}) collective-permute-start(f32[4,32,1280]{2,1,0:T(8,128)S(1)} %slice.9), channel_id=1, source_target_pairs={{0,24},{1,25},{2,26},{3,27},{4,196},{5,197},{6,198},{7,199},{8,0},... | collective-permute-start | bytes 1966088 | tf_op jit(solution)/shard_map/ppermute | solution.py:68
  69.0 5.3 %collective-permute-start.14 = (f32[8,32,1280]{2,1,0:T(8,128)S(1)}, f32[8,32,1280]{2,1,0:T(8,128)}, u32[]{:S(2)}, u32[]{:S(2)}) collective-permute-start(f32[8,32,1280]{2,1,0:T(8,128)S(1)} %collective-permute-done.9.c30), channel_id=1, source_target_pairs={{0,4},{1,5},{2,6},{3,7},{4,0},{5,1},{6,2},{7,3},{8,12},{9,13},{10,... | collective-permute-start | bytes 3932168 | tf_op jit(solution)/shard_map/ppermute | solution.py:68
  74.4 2.0 %collective-permute-done.11.db0 = f32[4,32,1280]{2,1,0:T(8,128)S(1)} collective-permute-done((f32[4,32,1280]{2,1,0:T(8,128)S(1)}, f32[4,32,1280]{2,1,0:T(8,128)S(1)}, u32[]{:S(2)}, u32[]{:S(2)}) %collective-permute-start.11) | collective-permute-done | bytes 655392 | tf_op jit(solution)/shard_map/ppermute | solution.py:68
  76.4 5.8 %collective-permute-start.16 = (f32[4,32,1280]{2,1,0:T(8,128)S(1)}, f32[4,32,1280]{2,1,0:T(8,128)}, u32[]{:S(2)}, u32[]{:S(2)}) collective-permute-start(f32[4,32,1280]{2,1,0:T(8,128)S(1)} %collective-permute-done.11.db0), channel_id=1, source_target_pairs={{0,4},{1,5},{2,6},{3,7},{4,0},{5,1},{6,2},{7,3},{8,12},{9,13},{10,... | collective-permute-start | bytes 1966088 | tf_op jit(solution)/shard_map/ppermute | solution.py:68
  82.2 3.9 %collective-permute-start.15 = (f32[4,32,1280]{2,1,0:T(8,128)}, f32[4,32,1280]{2,1,0:T(8,128)}, u32[]{:S(2)}, u32[]{:S(2)}) collective-permute-start(f32[4,32,1280]{2,1,0:T(8,128)} %collective-permute-done.10.da0), channel_id=1, source_target_pairs={{0,4},{1,5},{2,6},{3,7},{4,0},{5,1},{6,2},{7,3},{8,12},{9,13},{10,... | collective-permute-start | bytes 1966088 | tf_op jit(solution)/shard_map/ppermute | solution.py:68
  86.9 1.6 %copy-done = f32[1,1024,512]{2,1,0:T(8,128)S(1)} copy-done((f32[1,1024,512]{2,1,0:T(8,128)S(1)}, f32[1,1024,512]{2,1,0:T(8,128)}, u32[]{:S(2)}) %copy-start) | copy-done | bytes 2097176
  88.5 1.2 %copy-done.1 = f32[1,512,512]{2,1,0:T(8,128)S(1)} copy-done((f32[1,512,512]{2,1,0:T(8,128)S(1)}, f32[1,512,512]{2,1,0:T(8,128)}, u32[]{:S(2)}) %copy-start.1) | copy-done | bytes 1048600
  89.7 1.9 %update.1 = (bf16[512,1024]{1,0:T(8,128)(2,1)S(1)}, bf16[512,1024]{1,0:T(8,128)(2,1)S(1)}, f32[1,512]{1,0:T(1,128)S(1)}) custom-call(s32[1]{0:T(128)S(6)} %copy.12.width_ref, f32[1,512,512]{2,1,0:T(8,128)S(1)} %copy-done.1, f32[1,1024,512]{2,1,0:T(8,128)S(1)} %copy-done), custom_call_target="tpu_custom_call" | custom-call | flops 1610612736 | bytes 5242880 | tf_op jit(solution)/shard_map/update/pallas_call | solution.py:103
  91.7 21.3 %final.1 = (f32[1,1024,512]{2,1,0:T(8,128)}, f32[1,512]{1,0:T(1,128)}, f32[32,512]{1,0:T(8,128)}) custom-call(s32[5]{0:T(128)S(1)} %stack.47.where_ref, s32[1,8]{1,0:T(1,128)S(1)} %copy-done.2, bf16[512,1024]{1,0:T(8,128)(2,1)S(1)} %get-tuple-element.9.high_ref, bf16[512,1024]{1,0:T(8,128)(2,1)S(1)} %get-tuple-element.10.low_ref, ...), custom_call_target="tpu_custom_call" | custom-call | flops 10000000000 | bytes 20971520 | tf_op jit(solution)/shard_map/final/pallas_call | solution.py:267
  (30 shorter events, 2.9 us)
Async XLA Ops:
  0.6 0.7 collective-permute-start
  2.2 15.6 %collective-permute-start.3 = (f32[32,512]{1,0:T(8,128)S(1)}, f32[32,512]{1,0:T(8,128)S(1)}, u32[]{:S(2)}, u32[]{:S(2)}) collective-permute-start(f32[32,512]{1,0:T(8,128)S(1)} %broadcast_select_fusion), channel_id=1, source_target_pairs={{0,3},{1,0},{2,1},{3,2},{4,7},{5,4},{6,5},{7,6},{8,11},{9,8},{10,9... | collective-permute-start | bytes 196616 | tf_op jit(solution)/shard_map/ppermute | solution.py:68
  15.6 7.5 %collective-permute-start.2 = (f32[32,512]{1,0:T(8,128)S(1)}, f32[32,512]{1,0:T(8,128)S(1)}, u32[]{:S(2)}, u32[]{:S(2)}) collective-permute-start(f32[32,512]{1,0:T(8,128)S(1)} %broadcast_select_fusion), channel_id=1, source_target_pairs={{0,2},{1,3},{2,0},{3,1},{4,6},{5,7},{6,4},{7,5},{8,10},{9,11},{10,... | collective-permute-start | bytes 196616 | tf_op jit(solution)/shard_map/ppermute | solution.py:68
  15.6 7.5 %collective-permute-start.1 = (f32[32,512]{1,0:T(8,128)S(1)}, f32[32,512]{1,0:T(8,128)S(1)}, u32[]{:S(2)}, u32[]{:S(2)}) collective-permute-start(f32[32,512]{1,0:T(8,128)S(1)} %broadcast_select_fusion), channel_id=1, source_target_pairs={{0,1},{1,2},{2,3},{3,0},{4,5},{5,6},{6,7},{7,4},{8,9},{9,10},{10,1... | collective-permute-start | bytes 196616 | tf_op jit(solution)/shard_map/ppermute | solution.py:68
  23.8 5.4 %collective-permute-start.4 = (f32[32,1280]{1,0:T(8,128)S(1)}, f32[32,1280]{1,0:T(8,128)S(1)}, u32[]{:S(2)}, u32[]{:S(2)}) collective-permute-start(f32[32,1280]{1,0:T(8,128)S(1)} %get-tuple-element.16), channel_id=1, source_target_pairs={{0,32},{1,33},{2,34},{3,35},{4,39},{5,36},{6,37},{7,38},{8,40},{9,... | collective-permute-start | bytes 491528 | tf_op jit(solution)/shard_map/ppermute | solution.py:68
  29.2 15.3 %collective-permute-start.7 = (f32[2,32,1280]{2,1,0:T(8,128)S(1)}, f32[2,32,1280]{2,1,0:T(8,128)S(1)}, u32[]{:S(2)}, u32[]{:S(2)}) collective-permute-start(f32[2,32,1280]{2,1,0:T(8,128)S(1)} %pad_maximum_fusion), channel_id=1, source_target_pairs={{0,192},{1,193},{2,194},{3,195},{4,28},{5,29},{6,30},{7,31},{8,200... | collective-permute-start | bytes 983048 | tf_op jit(solution)/shard_map/ppermute | solution.py:68
  31.8 12.0 %collective-permute-start.6 = (f32[2,32,1280]{2,1,0:T(8,128)S(1)}, f32[2,32,1280]{2,1,0:T(8,128)S(1)}, u32[]{:S(2)}, u32[]{:S(2)}) collective-permute-start(f32[2,32,1280]{2,1,0:T(8,128)S(1)} %pad_maximum_fusion), channel_id=1, source_target_pairs={{0,128},{1,129},{2,130},{3,131},{4,20},{5,21},{6,22},{7,23},{8,136... | collective-permute-start | bytes 983048 | tf_op jit(solution)/shard_map/ppermute | solution.py:68
  32.3 10.7 %collective-permute-start.5 = (f32[2,32,1280]{2,1,0:T(8,128)S(1)}, f32[2,32,1280]{2,1,0:T(8,128)S(1)}, u32[]{:S(2)}, u32[]{:S(2)}) collective-permute-start(f32[2,32,1280]{2,1,0:T(8,128)S(1)} %pad_maximum_fusion), channel_id=1, source_target_pairs={{0,64},{1,65},{2,66},{3,67},{4,12},{5,13},{6,14},{7,15},{8,72},{9,... | collective-permute-start | bytes 983048 | tf_op jit(solution)/shard_map/ppermute | solution.py:68
  45.3 20.2 %collective-permute-start.9 = (f32[8,32,1280]{2,1,0:T(8,128)}, f32[8,32,1280]{2,1,0:T(8,128)S(1)}, u32[]{:S(2)}, u32[]{:S(2)}) collective-permute-start(f32[8,32,1280]{2,1,0:T(8,128)} %constant_dynamic-update-slice_fusion.q0), channel_id=1, source_target_pairs={{0,24},{1,25},{2,26},{3,27},{4,196},{5,197},{6,198},{7,199},{8,0},... | collective-permute-start | bytes 3932168 | tf_op jit(solution)/shard_map/ppermute | solution.py:68
  50.6 18.3 %collective-permute-start.8 = (f32[8,32,1280]{2,1,0:T(8,128)}, f32[8,32,1280]{2,1,0:T(8,128)S(1)}, u32[]{:S(2)}, u32[]{:S(2)}) collective-permute-start(f32[8,32,1280]{2,1,0:T(8,128)} %constant_dynamic-update-slice_fusion.q0), channel_id=1, source_target_pairs={{0,8},{1,9},{2,10},{3,11},{4,68},{5,69},{6,70},{7,71},{8,16},{9,17... | collective-permute-start | bytes 3932168 | tf_op jit(solution)/shard_map/ppermute | solution.py:68
  50.6 41.0 %collective-permute-start.12 = (f32[8,32,1280]{2,1,0:T(8,128)}, f32[8,32,1280]{2,1,0:T(8,128)}, u32[]{:S(2)}, u32[]{:S(2)}) collective-permute-start(f32[8,32,1280]{2,1,0:T(8,128)} %constant_dynamic-update-slice_fusion.q0), channel_id=1, source_target_pairs={{0,4},{1,5},{2,6},{3,7},{4,0},{5,1},{6,2},{7,3},{8,12},{9,13},{10,... | collective-permute-start | bytes 3932168 | tf_op jit(solution)/shard_map/ppermute | solution.py:68
  65.5 10.9 %collective-permute-start.11 = (f32[4,32,1280]{2,1,0:T(8,128)S(1)}, f32[4,32,1280]{2,1,0:T(8,128)S(1)}, u32[]{:S(2)}, u32[]{:S(2)}) collective-permute-start(f32[4,32,1280]{2,1,0:T(8,128)S(1)} %slice.9), channel_id=1, source_target_pairs={{0,24},{1,25},{2,26},{3,27},{4,196},{5,197},{6,198},{7,199},{8,0},... | collective-permute-start | bytes 1966088 | tf_op jit(solution)/shard_map/ppermute | solution.py:68
  68.9 13.3 %collective-permute-start.10 = (f32[4,32,1280]{2,1,0:T(8,128)S(1)}, f32[4,32,1280]{2,1,0:T(8,128)}, u32[]{:S(2)}, u32[]{:S(2)}) collective-permute-start(f32[4,32,1280]{2,1,0:T(8,128)S(1)} %slice.8), channel_id=1, source_target_pairs={{0,8},{1,9},{2,10},{3,11},{4,68},{5,69},{6,70},{7,71},{8,16},{9,17... | collective-permute-start | bytes 1966088 | tf_op jit(solution)/shard_map/ppermute | solution.py:68
  69.0 22.6 %collective-permute-start.14 = (f32[8,32,1280]{2,1,0:T(8,128)S(1)}, f32[8,32,1280]{2,1,0:T(8,128)}, u32[]{:S(2)}, u32[]{:S(2)}) collective-permute-start(f32[8,32,1280]{2,1,0:T(8,128)S(1)} %collective-permute-done.9.c30), channel_id=1, source_target_pairs={{0,4},{1,5},{2,6},{3,7},{4,0},{5,1},{6,2},{7,3},{8,12},{9,13},{10,... | collective-permute-start | bytes 3932168 | tf_op jit(solution)/shard_map/ppermute | solution.py:68
  74.3 17.3 %collective-permute-start.13 = (f32[8,32,1280]{2,1,0:T(8,128)S(1)}, f32[8,32,1280]{2,1,0:T(8,128)}, u32[]{:S(2)}, u32[]{:S(2)}) collective-permute-start(f32[8,32,1280]{2,1,0:T(8,128)S(1)} %collective-permute-done.8.c10), channel_id=1, source_target_pairs={{0,4},{1,5},{2,6},{3,7},{4,0},{5,1},{6,2},{7,3},{8,12},{9,13},{10,... | collective-permute-start | bytes 3932168 | tf_op jit(solution)/shard_map/ppermute | solution.py:68
  76.4 15.2 %collective-permute-start.16 = (f32[4,32,1280]{2,1,0:T(8,128)S(1)}, f32[4,32,1280]{2,1,0:T(8,128)}, u32[]{:S(2)}, u32[]{:S(2)}) collective-permute-start(f32[4,32,1280]{2,1,0:T(8,128)S(1)} %collective-permute-done.11.db0), channel_id=1, source_target_pairs={{0,4},{1,5},{2,6},{3,7},{4,0},{5,1},{6,2},{7,3},{8,12},{9,13},{10,... | collective-permute-start | bytes 1966088 | tf_op jit(solution)/shard_map/ppermute | solution.py:68
  82.2 9.4 %collective-permute-start.15 = (f32[4,32,1280]{2,1,0:T(8,128)}, f32[4,32,1280]{2,1,0:T(8,128)}, u32[]{:S(2)}, u32[]{:S(2)}) collective-permute-start(f32[4,32,1280]{2,1,0:T(8,128)} %collective-permute-done.10.da0), channel_id=1, source_target_pairs={{0,4},{1,5},{2,6},{3,7},{4,0},{5,1},{6,2},{7,3},{8,12},{9,13},{10,... | collective-permute-start | bytes 1966088 | tf_op jit(solution)/shard_map/ppermute | solution.py:68
  86.9 1.6 %copy-start = (f32[1,1024,512]{2,1,0:T(8,128)S(1)}, f32[1,1024,512]{2,1,0:T(8,128)}, u32[]{:S(2)}) copy-start(f32[1,1024,512]{2,1,0:T(8,128)} %panel_ref.1) | copy-start | bytes 6291460
  88.5 1.2 %copy-start.1 = (f32[1,512,512]{2,1,0:T(8,128)S(1)}, f32[1,512,512]{2,1,0:T(8,128)}, u32[]{:S(2)}) copy-start(f32[1,512,512]{2,1,0:T(8,128)} %inverse_ref.1) | copy-start | bytes 3145732
  89.7 2.0 %copy-start.2 = (s32[1,8]{1,0:T(1,128)S(1)}, s32[1,8]{1,0:T(1,128)}, u32[]{:S(2)}) copy-start(s32[1,8]{1,0:T(1,128)} %structure_ref.1) | copy-start | bytes 100

commit v2 on v1

v2 whole, which is shorter than its diff:
```python
import itertools

import jax
import jax.numpy as jnp
from jax import lax
from jax.experimental import pallas as pl
from jax.experimental.pallas import tpu as pltpu
from jax.sharding import PartitionSpec as P

AXES = ("col", "row")
F32 = jnp.float32
BF16 = jnp.bfloat16
NN = (((1,), (0,)), ((), ()))
NT = (((1,), (1,)), ((), ()))


def flat(y, zl, x, c, zh):
    return (((y * 2 + zl) * 4 + x) * 2 + c) * 4 + zh


def places():
    return itertools.product(range(4), range(2), range(4), range(2), range(4))


def pairs(move):
    found = []
    for place in places():
        target = move(*place)
        if target is not None:
            found.append((flat(*place), flat(*target)))
    return found


def fold_move(y, zl, x, c, zh):
    target = {(0, 1): (3, 1), (0, 2): (3, 2), (1, 2): (2, 1)}.get((y, zh))
    return None if target is None else (target[0], zl, x, c, target[1])


def plane_move(step):
    return lambda y, zl, x, c, zh: (y, zl, x, c, (zh + step) % 4)


def pair_move(y, zl, x, c, zh):
    z = zh * 2 + zl
    near = z ^ 1 if c == 0 else (z + (1 if z % 2 else -1)) % 8
    return (y, near % 2, x, c, near // 2)


def first_move(step):
    def move(y, zl, x, c, zh):
        return ((y + step) % 4, zl, x, c, zh) if c == 0 else (y, zl, (x + step) % 4, c, zh)

    return move


def second_move(step):
    def move(y, zl, x, c, zh):
        return (y, zl, (x + step) % 4, c, zh) if c == 0 else ((y + step) % 4, zl, x, c, zh)

    return move


def core_move(y, zl, x, c, zh):
    return (y, zl, x, 1 - c, zh)


def send(value, move):
    return lax.ppermute(value, AXES, pairs(move))


def halves(value):
    high = value.astype(BF16)
    return high, (value - high.astype(F32)).astype(BF16)


def dot3(ah, al, bh, bl, dims):
    def one(a, b):
        return lax.dot_general(a, b, dims, preferred_element_type=F32)

    return one(ah, bh) + (one(ah, bl) + one(al, bh))


def update_kernel(width_ref, inverse_ref, panel_ref, high_ref, low_ref, square_ref):
    width = width_ref[0]
    inverse = inverse_ref[0]
    rows = lax.broadcasted_iota(jnp.int32, inverse.shape, 0)
    cols = lax.broadcasted_iota(jnp.int32, inverse.shape, 1)
    inverse = jnp.where((rows < width) & (cols < width), inverse, 0.0)
    square_ref[...] = jnp.sum(inverse * inverse, axis=0, keepdims=True)
    inverse_high, inverse_low = halves(inverse.T)
    for part in range(4):
        panel = panel_ref[0, pl.ds(part * 256, 256), :]
        live = lax.broadcasted_iota(jnp.int32, panel.shape, 1) < width
        panel_high, panel_low = halves(jnp.where(live, panel, 0.0))
        update = dot3(inverse_high, inverse_low, panel_high, panel_low, NT)
        high, low = halves(update)
        high_ref[:, pl.ds(part * 256, 256)] = high
        low_ref[:, pl.ds(part * 256, 256)] = low


def update(widths, child_inverse, child_panel):
    vmem = pl.BlockSpec(memory_space=pltpu.VMEM)
    return pl.pallas_call(
        update_kernel,
        out_shape=(
            jax.ShapeDtypeStruct((512, 1024), BF16),
            jax.ShapeDtypeStruct((512, 1024), BF16),
            jax.ShapeDtypeStruct((1, 512), F32),
        ),
        in_specs=[pl.BlockSpec(memory_space=pltpu.SMEM), vmem, vmem],
        out_specs=(vmem, vmem, vmem),
        compiler_params=pltpu.CompilerParams(vmem_limit_bytes=12 * 2**20),
        cost_estimate=pl.CostEstimate(flops=6 * 1024 * 512 * 512, bytes_accessed=5 * 2**20, transcendentals=0),
        name="update",
    )(widths, child_inverse, child_panel)


VMEM = pl.BlockSpec(memory_space=pltpu.VMEM)
SMEM = pl.BlockSpec(memory_space=pltpu.SMEM)
EARLY, LATE = 768, 512
WIDE = EARLY + LATE


def limit(mebibytes):
    return pltpu.CompilerParams(vmem_limit_bytes=mebibytes * 2**20)


def line_kernel(where_ref, *refs):
    out = refs[-1]
    y0, zh0 = where_ref[0], where_ref[4]
    whole = jnp.minimum(y0, 2)
    half = jnp.where(y0 == 1, 2, 1)
    for d in range(4):
        source = refs[d]
        slot = (zh0 - d) & 3

        @pl.when(slot == 3)
        def _():
            out[:, EARLY:] = source[...]

        @pl.when((slot == whole) & (y0 < 2))
        def _():
            out[:, :512] = source[...]

        @pl.when((slot == half) & (y0 < 2))
        def _():
            out[:, 512:EARLY] = source[:, :256]

        @pl.when((slot == whole) & (y0 >= 2))
        def _():
            out[:, 256:EARLY] = source[...]

        @pl.when((slot == half) & (y0 >= 2))
        def _():
            out[:, :256] = source[:, 256:]


def make_line(where, planes):
    return pl.pallas_call(
        line_kernel,
        out_shape=jax.ShapeDtypeStruct((32, WIDE), F32),
        in_specs=[SMEM] + [VMEM] * 4,
        out_specs=VMEM,
        compiler_params=limit(2),
        name="line",
    )(where, *planes)


def join_kernel(*refs):
    out = refs[-1]
    start = 0
    for source in refs[:-1]:
        count = source.shape[0] if len(source.shape) == 3 else 1
        out[start : start + count] = source[...].reshape((count,) + out.shape[1:])
        start += count


def join(parts):
    count = sum(part.shape[0] if part.ndim == 3 else 1 for part in parts)
    return pl.pallas_call(
        join_kernel,
        out_shape=jax.ShapeDtypeStruct((count,) + parts[0].shape[-2:], F32),
        in_specs=[VMEM] * len(parts),
        out_specs=VMEM,
        compiler_params=limit(6),
        name="join",
    )(*parts)


def mix_kernel(left, right, quad, ahead, behind, aside):
    ahead[:2] = left[:2]
    ahead[2:] = quad[:2]
    behind[:2] = right[2:]
    behind[2:] = quad[2:]
    aside[:2] = left[2:]
    aside[2:] = right[:2]


def mix(left, right, quad):
    shape = jax.ShapeDtypeStruct((4, 32, WIDE), F32)
    return pl.pallas_call(
        mix_kernel,
        out_shape=(shape,) * 3,
        in_specs=[VMEM] * 3,
        out_specs=(VMEM,) * 3,
        compiler_params=limit(5),
        name="mix",
    )(left, right, quad)


def tails_kernel(ahead, behind, ahead_out, behind_out):
    ahead_out[...] = ahead[2:]
    behind_out[...] = behind[2:]


def tails(ahead, behind):
    shape = jax.ShapeDtypeStruct((2, 32, WIDE), F32)
    return pl.pallas_call(
        tails_kernel,
        out_shape=(shape,) * 2,
        in_specs=[VMEM] * 2,
        out_specs=(VMEM,) * 2,
        compiler_params=limit(4),
        name="tails",
    )(ahead, behind)


ROWS = 13 * 128
PLAN = (
    ((0, 768, 0, 0), (0, 768, 3, 768), (768, 512, 0, 1536)),
    ((0, 768, 1, 512), (0, 256, 2, 1280), (768, 512, 1, 1536)),
    ((256, 512, 2, 1024), (768, 512, 2, 1536)),
    ((768, 512, 3, 1536),),
)


def source_of(zr, d2, d1):
    if zr == 0:
        if d2 == 2:
            return (1, d1) if d1 < 2 else (1, 2 + d1)
        return 0, {0: 0, 1: 4, 3: 8}[d2] + d1
    if d2 == 0:
        return 0, 12 + d1
    if d2 == 1:
        return (1, 2 + d1) if d1 < 2 else (1, 6 + d1)
    if d2 == 3:
        return (1, 10 + d1) if d1 < 2 else (1, 4 + d1)
    return 2, d1


def lay_kernel(where_ref, structure_ref, near, side, other_near, other_side, ah, al, block_ref, table_ref):
    y0, zl0, x0, core0, zh0 = (where_ref[i] for i in range(5))
    for t in range(8):
        block_ref[t] = structure_ref[0, t]
    for t in range(4):
        block_ref[8 + t] = zh0 * 4 + t
    block_ref[12] = y0 * 4 + zl0 * 2 + x0 // 2
    for zr, d2, d1 in itertools.product(range(2), range(4), range(4)):
        array, index = source_of(zr, d2, d1)
        table_ref[zr * 16 + d2 * 4 + d1] = array * 16 + index

    def fill(*sources):
        def step(t, carry):
            block = block_ref[t]
            y, inner = block // 4, block & 3
            zr, xb = (inner // 2) ^ zl0, (inner & 1) * 2
            base = pl.multiple_of(t * 128, 128)

            def copy(part, lane, size, group, k):
                core = part & 1
                dy, dx = (y0 - group) & 3, (x0 - xb - part // 2) & 3
                d1, d2 = (dy, dx) if core == 0 else (dx, dy)
                first, second = sources[core]
                code = table_ref[zr * 16 + d2 * 4 + d1]
                index = code & 15
                lanes = slice(lane, lane + size)
                value = jnp.where(
                    code < 16, first[index, :, lanes], second[jnp.minimum(index, 11), :, lanes]
                )
                high, low = halves(value)
                row = pl.multiple_of(base + part * 32, 32)
                ah[pl.ds(row, 32), k : k + size] = high
                al[pl.ds(row, 32), k : k + size] = low

            for superblock in range(4):
                @pl.when(y == superblock)
                def _():
                    if superblock:
                        zero = jnp.zeros((128, 512 * superblock), BF16)
                        ah[pl.ds(base, 128), : 512 * superblock] = zero
                        al[pl.ds(base, 128), : 512 * superblock] = zero
                    for part in range(4):
                        for found in PLAN[superblock]:
                            copy(part, *found)

            return carry

        lax.fori_loop(0, 13, step, 0)

    @pl.when(core0 == 0)
    def _():
        fill((near, side), (other_near, other_side))

    @pl.when(core0 == 1)
    def _():
        fill((other_near, other_side), (near, side))


def lay(where, structure, pieces):
    shape = jax.ShapeDtypeStruct((ROWS, 2048), BF16)
    return pl.pallas_call(
        lay_kernel,
        out_shape=(shape, shape),
        in_specs=[SMEM, SMEM] + [VMEM] * 4,
        out_specs=(VMEM, VMEM),
        scratch_shapes=[pltpu.SMEM((16,), jnp.int32), pltpu.SMEM((32,), jnp.int32)],
        compiler_params=limit(25),
        cost_estimate=pl.CostEstimate(flops=10**10, bytes_accessed=10 * 2**20, transcendentals=0),
        name="lay",
    )(where, structure, *pieces)


FAR_PLAN = (
    ((0, 768, 0, 0), (768, 512, 0, 1536)),
    ((0, 768, 1, 512), (768, 512, 1, 1536)),
    ((0, 256, 1, 1280), (256, 512, 2, 1024), (768, 512, 2, 1536)),
    ((0, 768, 0, 768), (768, 512, 3, 1536)),
)


def patch(where_ref, structure_ref, slot_ref, far, other_far, ah, al):
    y0, zl0, x0, core0, zh0 = (where_ref[i] for i in range(5))
    for block in range(16):
        slot_ref[block] = -1
    for t in range(8):
        slot_ref[structure_ref[0, t]] = t

    def fill(source, core):
        def step(d1, carry):
            y = (y0 - jnp.where(core == 0, d1, 2)) & 3
            x = (x0 - jnp.where(core == 0, 2, d1)) & 3
            inner = (1 - zl0) * 2 + x // 2
            offset = (x & 1) * 64 + core * 32
            for group in range(4):
                @pl.when(y == group)
                def _():
                    for lane, size, superblock, k in FAR_PLAN[group]:
                        slot = slot_ref[superblock * 4 + inner]

                        def put(block):
                            row = pl.multiple_of(block * 128 + offset, 32)
                            high, low = halves(source[d1, :, lane : lane + size])
                            ah[pl.ds(row, 32), k : k + size] = high
                            al[pl.ds(row, 32), k : k + size] = low

                        @pl.when(slot >= 0)
                        def _():
                            put(slot)

                        @pl.when(zh0 == superblock)
                        def _():
                            put(8 + inner)

            return carry

        lax.fori_loop(0, 4, step, 0)

    fill(far, core0)
    fill(other_far, 1 - core0)


def final_kernel(
    where_ref, structure_ref, high_ref, low_ref, square_ref, ah, al, far, other_far,
    cross_ref, variance_ref, sigma_ref, slot_ref, th, tl, squares,
):
    patch(where_ref, structure_ref, slot_ref, far, other_far, ah, al)
    squares[...] = jnp.zeros_like(squares)

    def times(r, carry):
        k = pl.multiple_of(r * 256, 256)
        live = jnp.int32(0)
        for q in range(4):
            live += (structure_ref[0, 2 * q] < 2 * (r + 1)).astype(jnp.int32)

        @pl.when(live == 0)
        def _():
            zero = jnp.zeros((512, 256), BF16)
            th[:, pl.ds(k, 256)] = zero
            tl[:, pl.ds(k, 256)] = zero

        for v in range(1, 5):
            @pl.when(live == v)
            def _():
                depth = 256 * v
                total = dot3(
                    high_ref[:, :depth], low_ref[:, :depth],
                    ah[:depth, pl.ds(k, 256)], al[:depth, pl.ds(k, 256)], NN,
                )
                high, low = halves(total)
                th[:, pl.ds(k, 256)] = high
                tl[:, pl.ds(k, 256)] = low
                square = total * total
                squares[...] += square[:, :128] + square[:, 128:]

        return carry

    lax.fori_loop(0, 8, times, 0)

    def back(q, carry):
        row = pl.multiple_of(q * 256, 256)
        first = structure_ref[0, 2 * q] // 2
        for v in range(8):
            @pl.when(first == v)
            def _():
                k = 256 * v
                cross_ref[0, pl.ds(row, 256), :] = -dot3(
                    ah[pl.ds(row, 256), k:], al[pl.ds(row, 256), k:], th[:, k:], tl[:, k:], NT
                )

        return carry

    lax.fori_loop(0, 4, back, 0)
    variance_ref[...] = square_ref[...] + jnp.sum(squares[...].T, axis=0, keepdims=True)
    part = (where_ref[2] & 1) * 2 + where_ref[3]
    rows = pl.ds(pl.multiple_of(1536 + part * 32, 32), 32)
    sigma_ref[...] = dot3(ah[1024:1536, :], al[1024:1536, :], ah[rows, :], al[rows, :], NT).T


def final(where, structure, high, low, square, pieces):
    return pl.pallas_call(
        final_kernel,
        out_shape=(
            jax.ShapeDtypeStruct((1, 1024, 512), F32),
            jax.ShapeDtypeStruct((1, 512), F32),
            jax.ShapeDtypeStruct((32, 512), F32),
        ),
        in_specs=[SMEM, SMEM] + [VMEM] * 7,
        out_specs=(VMEM, VMEM, VMEM),
        scratch_shapes=[
            pltpu.SMEM((16,), jnp.int32),
            pltpu.VMEM((512, 2048), BF16), pltpu.VMEM((512, 2048), BF16),
            pltpu.VMEM((512, 128), F32),
        ],
        compiler_params=limit(26),
        cost_estimate=pl.CostEstimate(flops=10**10, bytes_accessed=10 * 2**20, transcendentals=0),
        name="final",
    )(where, structure, high, low, square, *pieces)


def body(root_inverse, child_inverse, child_panel, structure, widths):
    tie = lax.optimization_barrier
    col = lax.axis_index("col")
    zh0 = lax.axis_index("row")
    y0, zl0, x0, core0 = col // 16, (col // 8) % 2, (col // 2) % 4, col % 2
    where = jnp.stack([y0, zl0, x0, core0, zh0]).astype(jnp.int32)

    own = root_inverse.T
    folded = send(own, fold_move)
    moved = ((y0 == 3) & ((zh0 == 1) | (zh0 == 2))) | ((y0 == 2) & (zh0 == 1))
    own = jnp.where(moved, folded, own)
    planes = [own] + [send(own, plane_move(step)) for step in (1, 2, 3)]
    line = make_line(where, planes)

    quad = join([line] + [send(line, first_move(step)) for step in (1, 2, 3)])
    left, right = send(quad, second_move(1)), send(quad, second_move(3))
    quad_z = send(quad, pair_move)
    quad, child_inverse, child_panel = tie((quad, child_inverse, child_panel))
    high, low, square = update(widths, child_inverse, child_panel)
    left, right, quad_z, high, low, square = tie((left, right, quad_z, high, low, square))

    ahead, behind, aside = mix(left, right, quad_z)
    quad, left, right, quad_z, ahead, behind, aside = tie((quad, left, right, quad_z, ahead, behind, aside))
    ahead, behind, aside = send(ahead, second_move(1)), send(behind, second_move(3)), send(aside, pair_move)
    a = join([quad, left, right, quad_z])
    other_a = send(a, core_move)

    ahead_tail, behind_tail = tails(ahead, behind)
    ahead, behind, aside, ahead_tail, behind_tail = tie((ahead, behind, aside, ahead_tail, behind_tail))
    far = [send(ahead_tail, second_move(1)), send(behind_tail, second_move(3))]
    b = join([ahead, behind, aside])
    other_b = send(b, core_move)
    other_b, far = tie((other_b, far))
    ah, al = lay(where, structure, [a, b, other_a, other_b])
    c = join(far)
    other_c = send(c, core_move)
    cross, variance, sigma = final(where, structure, high, low, square, [ah, al, c, other_c])
    return sigma.T, cross, variance


def solution(mesh):
    placed = (
        P("row", "col"),
        P(("col", "row"), None, None),
        P(("col", "row"), None, None),
        P(("col", "row"), None),
        P(("col", "row")),
    )
    return jax.shard_map(
        body,
        mesh=mesh,
        in_specs=placed,
        out_specs=(P("row", "col"), P(("col", "row"), None, None), P(("col", "row"), None)),
        check_vma=False,
    )
```

time: 113 us -> 92.7 us (0.82)
  waiting for transfers between devices: 30.6 us -> 17.2 us
  local copies, waits for them, and re-layouts: 5.94 us -> 2.9 us
  starting transfers between devices: 50.2 us -> 48.5 us
    ppermute x17 -> x18, waiting for transfers between devices: 30.6 us -> 17.2 us  [send(): return lax.ppermute(value, AXES, pairs(move))]
    pallas_call x1, Pallas kernels: 21.3 us -> 15.3 us  [final(): pl.pallas_call(final_kernel, out_shape=(jax.ShapeDtypeStruct((1, 1024, 51...]
    pallas_call x0 -> x8, Pallas kernels: none -> 5.47 us  [the longest x1 4.27 us: lay(): pl.pallas_call(lay_kernel, out_shape=(shape, shape), in_specs=[SMEM, SMEM...]
    unnamed x9 -> x6, local copies, waits for them, and re-layouts: 5 us -> 2.81 us
    ppermute x17 -> x18, starting transfers between devices: 50.2 us -> 48.5 us  [send(): return lax.ppermute(value, AXES, pairs(move))]
  transfers between devices with their start and end apart: 17 -> 18, of which waited for: 5 -> 7; matrix products, arithmetic and copies ran while one was open for 2% -> 0% of each run, Pallas kernels for 2% -> 7%
where the time goes in v2:
time: 92.7 us; the launch traced here: 93.5 us
  starting transfers between devices  48.5 us (52%)
  Pallas kernels  22.6 us (24%)
  waiting for transfers between devices  17.2 us (19%)
  local copies, waits for them, and re-layouts  2.9 us (3%)
  between operations  1.45 us (2%)
    ppermute x18, starting transfers between devices, send(): return lax.ppermute(value, AXES, pairs(move))  48.5 us
    ppermute x18, waiting for transfers between devices, send(): return lax.ppermute(value, AXES, pairs(move))  17.2 us
    pallas_call x1, Pallas kernels, final(): pl.pallas_call(final_kernel, out_shape=(jax.ShapeDtypeStruct((1, 1024, 51...  15.3 us
    pallas_call x1, Pallas kernels, lay(): pl.pallas_call(lay_kernel, out_shape=(shape, shape), in_specs=[SMEM, SMEM...  4.27 us
    unnamed x6, local copies, waits for them, and re-layouts  2.81 us
    pallas_call x1, Pallas kernels, update(): pl.pallas_call(update_kernel, out_shape=(jax.ShapeDtypeStruct((512, 1024)...  1.89 us
  transfers between devices with their start and end apart: 18, of which 7 were waited for; matrix products, arithmetic and copies ran while one was open for 0% of the time, Pallas kernels for 7%

profile of v2, /device:TPU:1, one launch (start us, length us, event | category | flops | bytes accessed | tf_op | source)
XLA Modules:
  0.0 93.5 jit_solution(1282454908223709911)
XLA Ops:
  2.2 9.5 %collective-permute-start.1 = (f32[32,512]{1,0:T(8,128)S(1)}, f32[32,512]{1,0:T(8,128)S(1)}, u32[]{:S(2)}, u32[]{:S(2)}) collective-permute-start(f32[32,512]{1,0:T(8,128)S(1)} %broadcast_select_fusion.refs_0_), channel_id=1, source_target_pairs={{0,1},{1,2},{2,3},{3,0},{4,5},{5,6},{6,7},{7,4},{8,9},{9,10},{10,1... | collective-permute-start | bytes 196616 | tf_op jit(solution)/shard_map/ppermute | solution.py:68
  11.7 4.0 %collective-permute-start.2 = (f32[32,512]{1,0:T(8,128)S(1)}, f32[32,512]{1,0:T(8,128)S(1)}, u32[]{:S(2)}, u32[]{:S(2)}) collective-permute-start(f32[32,512]{1,0:T(8,128)S(1)} %broadcast_select_fusion.refs_0_), channel_id=1, source_target_pairs={{0,2},{1,3},{2,0},{3,1},{4,6},{5,7},{6,4},{7,5},{8,10},{9,11},{10,... | collective-permute-start | bytes 196616 | tf_op jit(solution)/shard_map/ppermute | solution.py:68
  15.7 3.5 %collective-permute-start.3 = (f32[32,512]{1,0:T(8,128)S(1)}, f32[32,512]{1,0:T(8,128)S(1)}, u32[]{:S(2)}, u32[]{:S(2)}) collective-permute-start(f32[32,512]{1,0:T(8,128)S(1)} %broadcast_select_fusion.refs_0_), channel_id=1, source_target_pairs={{0,3},{1,0},{2,1},{3,2},{4,7},{5,4},{6,5},{7,6},{8,11},{9,8},{10,9... | collective-permute-start | bytes 196616 | tf_op jit(solution)/shard_map/ppermute | solution.py:68
  19.2 1.8 %collective-permute-done.3.refs_3_ = f32[32,512]{1,0:T(8,128)S(1)} collective-permute-done((f32[32,512]{1,0:T(8,128)S(1)}, f32[32,512]{1,0:T(8,128)S(1)}, u32[]{:S(2)}, u32[]{:S(2)}) %collective-permute-start.3) | collective-permute-done | bytes 65568 | tf_op jit(solution)/shard_map/ppermute | solution.py:68
  21.7 1.3 %collective-permute-start.4 = (f32[32,1280]{1,0:T(8,128)S(1)}, f32[32,1280]{1,0:T(8,128)S(1)}, u32[]{:S(2)}, u32[]{:S(2)}) collective-permute-start(f32[32,1280]{1,0:T(8,128)S(1)} %line.1.refs_0_), channel_id=1, source_target_pairs={{0,64},{1,65},{2,66},{3,67},{4,12},{5,13},{6,14},{7,15},{8,72},{9,... | collective-permute-start | bytes 491528 | tf_op jit(solution)/shard_map/ppermute | solution.py:68
  23.0 2.5 %collective-permute-start.5 = (f32[32,1280]{1,0:T(8,128)S(1)}, f32[32,1280]{1,0:T(8,128)S(1)}, u32[]{:S(2)}, u32[]{:S(2)}) collective-permute-start(f32[32,1280]{1,0:T(8,128)S(1)} %line.1.refs_0_), channel_id=1, source_target_pairs={{0,128},{1,129},{2,130},{3,131},{4,20},{5,21},{6,22},{7,23},{8,136... | collective-permute-start | bytes 491528 | tf_op jit(solution)/shard_map/ppermute | solution.py:68
  27.2 2.7 %collective-permute-done.5.refs_2_ = f32[32,1280]{1,0:T(8,128)S(1)} collective-permute-done((f32[32,1280]{1,0:T(8,128)S(1)}, f32[32,1280]{1,0:T(8,128)S(1)}, u32[]{:S(2)}, u32[]{:S(2)}) %collective-permute-start.5) | collective-permute-done | bytes 163872 | tf_op jit(solution)/shard_map/ppermute | solution.py:68
  30.1 4.0 %collective-permute-start.8 = (f32[4,32,1280]{2,1,0:T(8,128)S(1)}, f32[4,32,1280]{2,1,0:T(8,128)S(1)}, u32[]{:S(2)}, u32[]{:S(2)}) collective-permute-start(f32[4,32,1280]{2,1,0:T(8,128)S(1)} %join.4.refs_0_), channel_id=1, source_target_pairs={{0,24},{1,25},{2,26},{3,27},{4,196},{5,197},{6,198},{7,199},{8,0},... | collective-permute-start | bytes 1966088 | tf_op jit(solution)/shard_map/ppermute | solution.py:68
  34.0 3.0 %collective-permute-start.9 = (f32[4,32,1280]{2,1,0:T(8,128)S(1)}, f32[4,32,1280]{2,1,0:T(8,128)S(1)}, u32[]{:S(2)}, u32[]{:S(2)}) collective-permute-start(f32[4,32,1280]{2,1,0:T(8,128)S(1)} %join.4.refs_0_), channel_id=1, source_target_pairs={{0,32},{1,33},{2,34},{3,35},{4,39},{5,36},{6,37},{7,38},{8,40},{9,... | collective-permute-start | bytes 1966088 | tf_op jit(solution)/shard_map/ppermute | solution.py:68
  37.7 1.6 %copy-done = f32[1,1024,512]{2,1,0:T(8,128)S(1)} copy-done((f32[1,1024,512]{2,1,0:T(8,128)S(1)}, f32[1,1024,512]{2,1,0:T(8,128)}, u32[]{:S(2)}) %copy-start) | copy-done | bytes 2097176
  39.3 1.2 %copy-done.1 = f32[1,512,512]{2,1,0:T(8,128)S(1)} copy-done((f32[1,512,512]{2,1,0:T(8,128)S(1)}, f32[1,512,512]{2,1,0:T(8,128)}, u32[]{:S(2)}) %copy-start.1) | copy-done | bytes 1048600
  40.5 1.9 %update.1 = (bf16[512,1024]{1,0:T(8,128)(2,1)S(1)}, bf16[512,1024]{1,0:T(8,128)(2,1)S(1)}, f32[1,512]{1,0:T(1,128)S(1)}) custom-call(s32[1]{0:T(128)S(6)} %copy.8.width_ref, f32[1,512,512]{2,1,0:T(8,128)S(1)} %copy-done.1, f32[1,1024,512]{2,1,0:T(8,128)S(1)} %copy-done), custom_call_target="tpu_custom_call" | custom-call | flops 1610612736 | bytes 5242880 | tf_op jit(solution)/shard_map/update/pallas_call | solution.py:103
  42.4 2.9 %collective-permute-done.9.quad.refs_3_ = f32[4,32,1280]{2,1,0:T(8,128)S(1)} collective-permute-done((f32[4,32,1280]{2,1,0:T(8,128)S(1)}, f32[4,32,1280]{2,1,0:T(8,128)S(1)}, u32[]{:S(2)}, u32[]{:S(2)}) %collective-permute-start.9) | collective-permute-done | bytes 655392 | tf_op jit(solution)/shard_map/ppermute | solution.py:68
  45.5 2.7 %collective-permute-start.11 = (f32[4,32,1280]{2,1,0:T(8,128)S(1)}, f32[4,32,1280]{2,1,0:T(8,128)S(1)}, u32[]{:S(2)}, u32[]{:S(2)}) collective-permute-start(f32[4,32,1280]{2,1,0:T(8,128)S(1)} %get-tuple-element.60), channel_id=1, source_target_pairs={{0,24},{1,25},{2,26},{3,27},{4,196},{5,197},{6,198},{7,199},{8,0},... | collective-permute-start | bytes 1966088 | tf_op jit(solution)/shard_map/ppermute | solution.py:68
  48.2 2.7 %collective-permute-start.12 = (f32[4,32,1280]{2,1,0:T(8,128)S(1)}, f32[4,32,1280]{2,1,0:T(8,128)S(1)}, u32[]{:S(2)}, u32[]{:S(2)}) collective-permute-start(f32[4,32,1280]{2,1,0:T(8,128)S(1)} %get-tuple-element.61), channel_id=1, source_target_pairs={{0,32},{1,33},{2,34},{3,35},{4,39},{5,36},{6,37},{7,38},{8,40},{9,... | collective-permute-start | bytes 1966088 | tf_op jit(solution)/shard_map/ppermute | solution.py:68
  51.0 3.7 %collective-permute-start.13 = (f32[16,32,1280]{2,1,0:T(8,128)S(1)}, f32[16,32,1280]{2,1,0:T(8,128)S(1)}, u32[]{:S(2)}, u32[]{:S(2)}) collective-permute-start(f32[16,32,1280]{2,1,0:T(8,128)S(1)} %join.5.near), channel_id=1, source_target_pairs={{0,4},{1,5},{2,6},{3,7},{4,0},{5,1},{6,2},{7,3},{8,12},{9,13},{10,... | collective-permute-start | bytes 7864328 | tf_op jit(solution)/shard_map/ppermute | solution.py:68
  54.7 1.7 %collective-permute-done.10.ahead.refs_0_ = f32[4,32,1280]{2,1,0:T(8,128)S(1)} collective-permute-done((f32[4,32,1280]{2,1,0:T(8,128)S(1)}, f32[4,32,1280]{2,1,0:T(8,128)S(1)}, u32[]{:S(2)}, u32[]{:S(2)}) %collective-permute-start.10) | collective-permute-done | bytes 655392 | tf_op jit(solution)/shard_map/ppermute | solution.py:68
  56.5 2.6 %collective-permute-done.12.refs_2_ = f32[4,32,1280]{2,1,0:T(8,128)S(1)} collective-permute-done((f32[4,32,1280]{2,1,0:T(8,128)S(1)}, f32[4,32,1280]{2,1,0:T(8,128)S(1)}, u32[]{:S(2)}, u32[]{:S(2)}) %collective-permute-start.12) | collective-permute-done | bytes 655392 | tf_op jit(solution)/shard_map/ppermute | solution.py:68
  59.3 6.0 %collective-permute-start.14 = (f32[12,32,1280]{2,1,0:T(8,128)S(1)}, f32[12,32,1280]{2,1,0:T(8,128)S(1)}, u32[]{:S(2)}, u32[]{:S(2)}) collective-permute-start(f32[12,32,1280]{2,1,0:T(8,128)S(1)} %join.6.side), channel_id=1, source_target_pairs={{0,4},{1,5},{2,6},{3,7},{4,0},{5,1},{6,2},{7,3},{8,12},{9,13},{10,... | collective-permute-start | bytes 5898248 | tf_op jit(solution)/shard_map/ppermute | solution.py:68
  65.3 2.7 %collective-permute-start.16 = (f32[2,32,1280]{2,1,0:T(8,128)S(1)}, f32[2,32,1280]{2,1,0:T(8,128)S(1)}, u32[]{:S(2)}, u32[]{:S(2)}) collective-permute-start(f32[2,32,1280]{2,1,0:T(8,128)S(1)} %get-tuple-element.68), channel_id=1, source_target_pairs={{0,24},{1,25},{2,26},{3,27},{4,196},{5,197},{6,198},{7,199},{8,0},... | collective-permute-start | bytes 983048 | tf_op jit(solution)/shard_map/ppermute | solution.py:68
  67.9 4.8 %collective-permute-done.15.refs_0_ = f32[2,32,1280]{2,1,0:T(8,128)S(1)} collective-permute-done((f32[2,32,1280]{2,1,0:T(8,128)S(1)}, f32[2,32,1280]{2,1,0:T(8,128)S(1)}, u32[]{:S(2)}, u32[]{:S(2)}) %collective-permute-start.15) | collective-permute-done | bytes 327712 | tf_op jit(solution)/shard_map/ppermute | solution.py:68
  72.8 1.2 %collective-permute-start.17 = (f32[4,32,1280]{2,1,0:T(8,128)S(1)}, f32[4,32,1280]{2,1,0:T(8,128)S(1)}, u32[]{:S(2)}, u32[]{:S(2)}) collective-permute-start(f32[4,32,1280]{2,1,0:T(8,128)S(1)} %join.7.far), channel_id=1, source_target_pairs={{0,4},{1,5},{2,6},{3,7},{4,0},{5,1},{6,2},{7,3},{8,12},{9,13},{10,... | collective-permute-start | bytes 1966088 | tf_op jit(solution)/shard_map/ppermute | solution.py:68
  74.0 4.3 %lay.1 = (bf16[1664,2048]{1,0:T(8,128)(2,1)S(1)}, bf16[1664,2048]{1,0:T(8,128)(2,1)S(1)}) custom-call(s32[5]{0:T(128)S(1)} %stack.23.where_ref, s32[1,8]{1,0:T(1,128)S(1)} %copy-done.2, f32[16,32,1280]{2,1,0:T(8,128)S(1)} %join.5.near, f32[12,32,1280]{2,1,0:T(8,128)S(1)} %join.6.side, f32[16,32,1280]{2,1,0:T(8,128)S(1)} %collective-permute-done.13.other_near, ...), custom_call_target="tpu_custom_call" | custom-call | flops 10000000000 | bytes 10485760 | tf_op jit(solution)/shard_map/lay/pallas_call | solution.py:311
  78.3 15.3 %final.1 = (f32[1,1024,512]{2,1,0:T(8,128)}, f32[1,512]{1,0:T(1,128)}, f32[32,512]{1,0:T(8,128)}) custom-call(s32[5]{0:T(128)S(1)} %stack.23.where_ref, s32[1,8]{1,0:T(1,128)S(1)} %copy-done.2, bf16[512,1024]{1,0:T(8,128)(2,1)S(1)} %get-tuple-element.45.high_ref, bf16[512,1024]{1,0:T(8,128)(2,1)S(1)} %get-tuple-element.46.low_ref, ...), custom_call_target="tpu_custom_call" | custom-call | flops 10000000000 | bytes 10485760 | tf_op jit(solution)/shard_map/final/pallas_call | solution.py:430
  (30 shorter events, 4.7 us)
Async XLA Ops:
  0.6 0.7 collective-permute-start
  2.2 17.0 %collective-permute-start.1 = (f32[32,512]{1,0:T(8,128)S(1)}, f32[32,512]{1,0:T(8,128)S(1)}, u32[]{:S(2)}, u32[]{:S(2)}) collective-permute-start(f32[32,512]{1,0:T(8,128)S(1)} %broadcast_select_fusion.refs_0_), channel_id=1, source_target_pairs={{0,1},{1,2},{2,3},{3,0},{4,5},{5,6},{6,7},{7,4},{8,9},{9,10},{10,1... | collective-permute-start | bytes 196616 | tf_op jit(solution)/shard_map/ppermute | solution.py:68
  11.7 7.6 %collective-permute-start.2 = (f32[32,512]{1,0:T(8,128)S(1)}, f32[32,512]{1,0:T(8,128)S(1)}, u32[]{:S(2)}, u32[]{:S(2)}) collective-permute-start(f32[32,512]{1,0:T(8,128)S(1)} %broadcast_select_fusion.refs_0_), channel_id=1, source_target_pairs={{0,2},{1,3},{2,0},{3,1},{4,6},{5,7},{6,4},{7,5},{8,10},{9,11},{10,... | collective-permute-start | bytes 196616 | tf_op jit(solution)/shard_map/ppermute | solution.py:68
  15.7 5.4 %collective-permute-start.3 = (f32[32,512]{1,0:T(8,128)S(1)}, f32[32,512]{1,0:T(8,128)S(1)}, u32[]{:S(2)}, u32[]{:S(2)}) collective-permute-start(f32[32,512]{1,0:T(8,128)S(1)} %broadcast_select_fusion.refs_0_), channel_id=1, source_target_pairs={{0,3},{1,0},{2,1},{3,2},{4,7},{5,4},{6,5},{7,6},{8,11},{9,8},{10,9... | collective-permute-start | bytes 196616 | tf_op jit(solution)/shard_map/ppermute | solution.py:68
  21.7 5.5 %collective-permute-start.4 = (f32[32,1280]{1,0:T(8,128)S(1)}, f32[32,1280]{1,0:T(8,128)S(1)}, u32[]{:S(2)}, u32[]{:S(2)}) collective-permute-start(f32[32,1280]{1,0:T(8,128)S(1)} %line.1.refs_0_), channel_id=1, source_target_pairs={{0,64},{1,65},{2,66},{3,67},{4,12},{5,13},{6,14},{7,15},{8,72},{9,... | collective-permute-start | bytes 491528 | tf_op jit(solution)/shard_map/ppermute | solution.py:68
  23.0 6.9 %collective-permute-start.5 = (f32[32,1280]{1,0:T(8,128)S(1)}, f32[32,1280]{1,0:T(8,128)S(1)}, u32[]{:S(2)}, u32[]{:S(2)}) collective-permute-start(f32[32,1280]{1,0:T(8,128)S(1)} %line.1.refs_0_), channel_id=1, source_target_pairs={{0,128},{1,129},{2,130},{3,131},{4,20},{5,21},{6,22},{7,23},{8,136... | collective-permute-start | bytes 491528 | tf_op jit(solution)/shard_map/ppermute | solution.py:68
  25.5 4.5 %collective-permute-start.6 = (f32[32,1280]{1,0:T(8,128)S(1)}, f32[32,1280]{1,0:T(8,128)S(1)}, u32[]{:S(2)}, u32[]{:S(2)}) collective-permute-start(f32[32,1280]{1,0:T(8,128)S(1)} %line.1.refs_0_), channel_id=1, source_target_pairs={{0,192},{1,193},{2,194},{3,195},{4,28},{5,29},{6,30},{7,31},{8,200... | collective-permute-start | bytes 491528 | tf_op jit(solution)/shard_map/ppermute | solution.py:68
  30.0 12.4 %collective-permute-start.7 = (f32[4,32,1280]{2,1,0:T(8,128)S(1)}, f32[4,32,1280]{2,1,0:T(8,128)S(1)}, u32[]{:S(2)}, u32[]{:S(2)}) collective-permute-start(f32[4,32,1280]{2,1,0:T(8,128)S(1)} %join.4.refs_0_), channel_id=1, source_target_pairs={{0,8},{1,9},{2,10},{3,11},{4,68},{5,69},{6,70},{7,71},{8,16},{9,17... | collective-permute-start | bytes 1966088 | tf_op jit(solution)/shard_map/ppermute | solution.py:68
  30.1 12.3 %collective-permute-start.8 = (f32[4,32,1280]{2,1,0:T(8,128)S(1)}, f32[4,32,1280]{2,1,0:T(8,128)S(1)}, u32[]{:S(2)}, u32[]{:S(2)}) collective-permute-start(f32[4,32,1280]{2,1,0:T(8,128)S(1)} %join.4.refs_0_), channel_id=1, source_target_pairs={{0,24},{1,25},{2,26},{3,27},{4,196},{5,197},{6,198},{7,199},{8,0},... | collective-permute-start | bytes 1966088 | tf_op jit(solution)/shard_map/ppermute | solution.py:68
  34.0 11.3 %collective-permute-start.9 = (f32[4,32,1280]{2,1,0:T(8,128)S(1)}, f32[4,32,1280]{2,1,0:T(8,128)S(1)}, u32[]{:S(2)}, u32[]{:S(2)}) collective-permute-start(f32[4,32,1280]{2,1,0:T(8,128)S(1)} %join.4.refs_0_), channel_id=1, source_target_pairs={{0,32},{1,33},{2,34},{3,35},{4,39},{5,36},{6,37},{7,38},{8,40},{9,... | collective-permute-start | bytes 1966088 | tf_op jit(solution)/shard_map/ppermute | solution.py:68
  37.7 1.6 %copy-start = (f32[1,1024,512]{2,1,0:T(8,128)S(1)}, f32[1,1024,512]{2,1,0:T(8,128)}, u32[]{:S(2)}) copy-start(f32[1,1024,512]{2,1,0:T(8,128)} %panel_ref) | copy-start | bytes 6291460
  39.3 1.2 %copy-start.1 = (f32[1,512,512]{2,1,0:T(8,128)S(1)}, f32[1,512,512]{2,1,0:T(8,128)}, u32[]{:S(2)}) copy-start(f32[1,512,512]{2,1,0:T(8,128)} %inverse_ref) | copy-start | bytes 3145732
  45.4 11.0 %collective-permute-start.10 = (f32[4,32,1280]{2,1,0:T(8,128)S(1)}, f32[4,32,1280]{2,1,0:T(8,128)S(1)}, u32[]{:S(2)}, u32[]{:S(2)}) collective-permute-start(f32[4,32,1280]{2,1,0:T(8,128)S(1)} %get-tuple-element.59), channel_id=1, source_target_pairs={{0,8},{1,9},{2,10},{3,11},{4,68},{5,69},{6,70},{7,71},{8,16},{9,17... | collective-permute-start | bytes 1966088 | tf_op jit(solution)/shard_map/ppermute | solution.py:68
  45.5 10.9 %collective-permute-start.11 = (f32[4,32,1280]{2,1,0:T(8,128)S(1)}, f32[4,32,1280]{2,1,0:T(8,128)S(1)}, u32[]{:S(2)}, u32[]{:S(2)}) collective-permute-start(f32[4,32,1280]{2,1,0:T(8,128)S(1)} %get-tuple-element.60), channel_id=1, source_target_pairs={{0,24},{1,25},{2,26},{3,27},{4,196},{5,197},{6,198},{7,199},{8,0},... | collective-permute-start | bytes 1966088 | tf_op jit(solution)/shard_map/ppermute | solution.py:68
  48.2 10.9 %collective-permute-start.12 = (f32[4,32,1280]{2,1,0:T(8,128)S(1)}, f32[4,32,1280]{2,1,0:T(8,128)S(1)}, u32[]{:S(2)}, u32[]{:S(2)}) collective-permute-start(f32[4,32,1280]{2,1,0:T(8,128)S(1)} %get-tuple-element.61), channel_id=1, source_target_pairs={{0,32},{1,33},{2,34},{3,35},{4,39},{5,36},{6,37},{7,38},{8,40},{9,... | collective-permute-start | bytes 1966088 | tf_op jit(solution)/shard_map/ppermute | solution.py:68
  51.0 22.9 %collective-permute-start.13 = (f32[16,32,1280]{2,1,0:T(8,128)S(1)}, f32[16,32,1280]{2,1,0:T(8,128)S(1)}, u32[]{:S(2)}, u32[]{:S(2)}) collective-permute-start(f32[16,32,1280]{2,1,0:T(8,128)S(1)} %join.5.near), channel_id=1, source_target_pairs={{0,4},{1,5},{2,6},{3,7},{4,0},{5,1},{6,2},{7,3},{8,12},{9,13},{10,... | collective-permute-start | bytes 7864328 | tf_op jit(solution)/shard_map/ppermute | solution.py:68
  59.1 14.8 %copy-start.2 = (s32[1,8]{1,0:T(1,128)S(1)}, s32[1,8]{1,0:T(1,128)}, u32[]{:S(2)}) copy-start(s32[1,8]{1,0:T(1,128)} %structure_ref.3) | copy-start | bytes 100
  59.3 13.4 %collective-permute-start.14 = (f32[12,32,1280]{2,1,0:T(8,128)S(1)}, f32[12,32,1280]{2,1,0:T(8,128)S(1)}, u32[]{:S(2)}, u32[]{:S(2)}) collective-permute-start(f32[12,32,1280]{2,1,0:T(8,128)S(1)} %join.6.side), channel_id=1, source_target_pairs={{0,4},{1,5},{2,6},{3,7},{4,0},{5,1},{6,2},{7,3},{8,12},{9,13},{10,... | collective-permute-start | bytes 5898248 | tf_op jit(solution)/shard_map/ppermute | solution.py:68
  65.3 7.4 %collective-permute-start.15 = (f32[2,32,1280]{2,1,0:T(8,128)S(1)}, f32[2,32,1280]{2,1,0:T(8,128)S(1)}, u32[]{:S(2)}, u32[]{:S(2)}) collective-permute-start(f32[2,32,1280]{2,1,0:T(8,128)S(1)} %get-tuple-element.67), channel_id=1, source_target_pairs={{0,8},{1,9},{2,10},{3,11},{4,68},{5,69},{6,70},{7,71},{8,16},{9,17... | collective-permute-start | bytes 983048 | tf_op jit(solution)/shard_map/ppermute | solution.py:68
  65.3 7.4 %collective-permute-start.16 = (f32[2,32,1280]{2,1,0:T(8,128)S(1)}, f32[2,32,1280]{2,1,0:T(8,128)S(1)}, u32[]{:S(2)}, u32[]{:S(2)}) collective-permute-start(f32[2,32,1280]{2,1,0:T(8,128)S(1)} %get-tuple-element.68), channel_id=1, source_target_pairs={{0,24},{1,25},{2,26},{3,27},{4,196},{5,197},{6,198},{7,199},{8,0},... | collective-permute-start | bytes 983048 | tf_op jit(solution)/shard_map/ppermute | solution.py:68
  72.8 5.5 %collective-permute-start.17 = (f32[4,32,1280]{2,1,0:T(8,128)S(1)}, f32[4,32,1280]{2,1,0:T(8,128)S(1)}, u32[]{:S(2)}, u32[]{:S(2)}) collective-permute-start(f32[4,32,1280]{2,1,0:T(8,128)S(1)} %join.7.far), channel_id=1, source_target_pairs={{0,4},{1,5},{2,6},{3,7},{4,0},{5,1},{6,2},{7,3},{8,12},{9,13},{10,... | collective-permute-start | bytes 1966088 | tf_op jit(solution)/shard_map/ppermute | solution.py:68

commit v3 on v2

--- a/solution.py
+++ b/solution.py
@@ -32,8 +32,9 @@
 
 
 def fold_move(y, zl, x, c, zh):
-    target = {(0, 1): (3, 1), (0, 2): (3, 2), (1, 2): (2, 1)}.get((y, zh))
-    return None if target is None else (target[0], zl, x, c, target[1])
+    swaps = {(0, 1): (3, 1), (0, 2): (3, 2), (1, 2): (2, 1), (3, 1): (0, 1), (3, 2): (0, 2), (2, 1): (1, 2)}
+    target = swaps.get((y, zh), (y, zh))
+    return (target[0], zl, x, c, target[1])
 
 
 def plane_move(step):
@@ -371,7 +372,7 @@
 
 def final_kernel(
     where_ref, structure_ref, high_ref, low_ref, square_ref, ah, al, far, other_far,
-    cross_ref, variance_ref, sigma_ref, slot_ref, th, tl, squares,
+    cross_ref, variance_ref, sigma_ref, slot_ref, th, tl, squares, result, pair, sums, done,
 ):
     patch(where_ref, structure_ref, slot_ref, far, other_far, ah, al)
     squares[...] = jnp.zeros_like(squares)
@@ -413,17 +414,34 @@
             @pl.when(first == v)
             def _():
                 k = 256 * v
-                cross_ref[0, pl.ds(row, 256), :] = -dot3(
+                result[pl.ds(row, 256), :] = -dot3(
                     ah[pl.ds(row, 256), k:], al[pl.ds(row, 256), k:], th[:, k:], tl[:, k:], NT
                 )
 
+        leave(q).start()
         return carry
+
+    def leave(q):
+        rows = pl.ds(pl.multiple_of(q * 256, 256), 256)
+        return pltpu.make_async_copy(result.at[rows, :], cross_ref.at[0, rows, :], done.at[q])
 
     lax.fori_loop(0, 4, back, 0)
     variance_ref[...] = square_ref[...] + jnp.sum(squares[...].T, axis=0, keepdims=True)
     part = (where_ref[2] & 1) * 2 + where_ref[3]
     rows = pl.ds(pl.multiple_of(1536 + part * 32, 32), 32)
-    sigma_ref[...] = dot3(ah[1024:1536, :], al[1024:1536, :], ah[rows, :], al[rows, :], NT).T
+    pair[:32] = ah[rows, :]
+    pair[32:] = al[rows, :]
+    for v in range(4):
+        @pl.when(jnp.maximum(where_ref[0], where_ref[4]) == v)
+        def _():
+            k = 512 * v
+            wide = lax.dot_general(ah[1024:1536, k:], pair[:, k:], NT, preferred_element_type=F32)
+            rest = lax.dot_general(al[1024:1536, k:], pair[:32, k:], NT, preferred_element_type=F32)
+            sums[...] = wide[:, :32] + (wide[:, 32:] + rest)
+
+    sigma_ref[...] = sums[...].T
+    for q in range(4):
+        leave(q).wait()
 
 
 def final(where, structure, high, low, square, pieces):
@@ -435,11 +453,13 @@
             jax.ShapeDtypeStruct((32, 512), F32),
         ),
         in_specs=[SMEM, SMEM] + [VMEM] * 7,
-        out_specs=(VMEM, VMEM, VMEM),
+        out_specs=(pl.BlockSpec(memory_space=pl.ANY), VMEM, VMEM),
         scratch_shapes=[
             pltpu.SMEM((16,), jnp.int32),
             pltpu.VMEM((512, 2048), BF16), pltpu.VMEM((512, 2048), BF16),
-            pltpu.VMEM((512, 128), F32),
+            pltpu.VMEM((512, 128), F32), pltpu.VMEM((1024, 512), F32),
+            pltpu.VMEM((64, 2048), BF16), pltpu.VMEM((512, 32), F32),
+            pltpu.SemaphoreType.DMA((4,)),
         ],
         compiler_params=limit(26),
         cost_estimate=pl.CostEstimate(flops=10**10, bytes_accessed=10 * 2**20, transcendentals=0),

time: 92.7 us -> 92.3 us (level); the launches traced: 93.5 us -> 90.7 us
  starting transfers between devices: 48.5 us -> 45.3 us
  waiting for transfers between devices: 17.2 us -> 19.1 us
  Pallas kernels: 22.6 us -> 21 us
    ppermute x18, starting transfers between devices: 48.5 us -> 45.3 us  [send(): return lax.ppermute(value, AXES, pairs(move))]
    ppermute x18, waiting for transfers between devices: 17.2 us -> 19.1 us  [send(): return lax.ppermute(value, AXES, pairs(move))]
    pallas_call x1, Pallas kernels: 15.3 us -> 13.9 us  [final(): pl.pallas_call(final_kernel, out_shape=(jax.ShapeDtypeStruct((1, 1024, 51...]
  transfers between devices with their start and end apart: 18 -> 18, of which waited for: 7 -> 9; matrix products, arithmetic and copies ran while one was open for 0% -> 0% of each run, Pallas kernels for 7% -> 7%
where the time goes in v3:
time: 92.3 us; the launch traced here: 90.7 us
  starting transfers between devices  45.3 us (49%)
  Pallas kernels  21 us (23%)
  waiting for transfers between devices  19.1 us (21%)
  local copies, waits for them, and re-layouts  2.9 us (3%)
  between operations  1.56 us (2%)
    ppermute x18, starting transfers between devices, send(): return lax.ppermute(value, AXES, pairs(move))  45.3 us
    ppermute x18, waiting for transfers between devices, send(): return lax.ppermute(value, AXES, pairs(move))  19.1 us
    pallas_call x1, Pallas kernels, final(): pl.pallas_call(final_kernel, out_shape=(jax.ShapeDtypeStruct((1, 1024, 51...  13.9 us
    pallas_call x1, Pallas kernels, lay(): pl.pallas_call(lay_kernel, out_shape=(shape, shape), in_specs=[SMEM, SMEM...  4.06 us
    unnamed x6, local copies, waits for them, and re-layouts  2.81 us
    pallas_call x1, Pallas kernels, update(): pl.pallas_call(update_kernel, out_shape=(jax.ShapeDtypeStruct((512, 1024)...  1.89 us
  transfers between devices with their start and end apart: 18, of which 9 were waited for; matrix products, arithmetic and copies ran while one was open for 0% of the time, Pallas kernels for 7%

profile of v3, /device:TPU:1, one launch (start us, length us, event | category | flops | bytes accessed | tf_op | source)
XLA Modules:
  0.0 90.7 jit_solution(337627563739204258)
XLA Ops:
  0.6 1.5 %collective-permute-start = (f32[32,512]{1,0:T(8,128)}, f32[32,512]{1,0:T(8,128)S(1)}, u32[]{:S(2)}, u32[]{:S(2)}) collective-permute-start(f32[32,512]{1,0:T(8,128)} %bitcast.8), channel_id=1, source_target_pairs={{0,0},{1,193},{2,194},{3,3},{4,4},{5,197},{6,198},{7,7},{8,8},{9,2... | collective-permute-start | bytes 196616 | tf_op jit(solution)/shard_map/ppermute | solution.py:69
  3.0 8.9 %collective-permute-start.1 = (f32[32,512]{1,0:T(8,128)S(1)}, f32[32,512]{1,0:T(8,128)S(1)}, u32[]{:S(2)}, u32[]{:S(2)}) collective-permute-start(f32[32,512]{1,0:T(8,128)S(1)} %broadcast_select_fusion.refs_0_), channel_id=1, source_target_pairs={{0,1},{1,2},{2,3},{3,0},{4,5},{5,6},{6,7},{7,4},{8,9},{9,10},{10,1... | collective-permute-start | bytes 196616 | tf_op jit(solution)/shard_map/ppermute | solution.py:69
  11.9 4.0 %collective-permute-start.2 = (f32[32,512]{1,0:T(8,128)S(1)}, f32[32,512]{1,0:T(8,128)S(1)}, u32[]{:S(2)}, u32[]{:S(2)}) collective-permute-start(f32[32,512]{1,0:T(8,128)S(1)} %broadcast_select_fusion.refs_0_), channel_id=1, source_target_pairs={{0,2},{1,3},{2,0},{3,1},{4,6},{5,7},{6,4},{7,5},{8,10},{9,11},{10,... | collective-permute-start | bytes 196616 | tf_op jit(solution)/shard_map/ppermute | solution.py:69
  15.9 3.5 %collective-permute-start.3 = (f32[32,512]{1,0:T(8,128)S(1)}, f32[32,512]{1,0:T(8,128)S(1)}, u32[]{:S(2)}, u32[]{:S(2)}) collective-permute-start(f32[32,512]{1,0:T(8,128)S(1)} %broadcast_select_fusion.refs_0_), channel_id=1, source_target_pairs={{0,3},{1,0},{2,1},{3,2},{4,7},{5,4},{6,5},{7,6},{8,11},{9,8},{10,9... | collective-permute-start | bytes 196616 | tf_op jit(solution)/shard_map/ppermute | solution.py:69
  19.5 1.9 %collective-permute-done.3.refs_3_ = f32[32,512]{1,0:T(8,128)S(1)} collective-permute-done((f32[32,512]{1,0:T(8,128)S(1)}, f32[32,512]{1,0:T(8,128)S(1)}, u32[]{:S(2)}, u32[]{:S(2)}) %collective-permute-start.3) | collective-permute-done | bytes 65568 | tf_op jit(solution)/shard_map/ppermute | solution.py:69
  22.0 1.3 %collective-permute-start.4 = (f32[32,1280]{1,0:T(8,128)S(1)}, f32[32,1280]{1,0:T(8,128)S(1)}, u32[]{:S(2)}, u32[]{:S(2)}) collective-permute-start(f32[32,1280]{1,0:T(8,128)S(1)} %line.1.refs_0_), channel_id=1, source_target_pairs={{0,64},{1,65},{2,66},{3,67},{4,12},{5,13},{6,14},{7,15},{8,72},{9,... | collective-permute-start | bytes 491528 | tf_op jit(solution)/shard_map/ppermute | solution.py:69
  23.3 2.5 %collective-permute-start.5 = (f32[32,1280]{1,0:T(8,128)S(1)}, f32[32,1280]{1,0:T(8,128)S(1)}, u32[]{:S(2)}, u32[]{:S(2)}) collective-permute-start(f32[32,1280]{1,0:T(8,128)S(1)} %line.1.refs_0_), channel_id=1, source_target_pairs={{0,128},{1,129},{2,130},{3,131},{4,20},{5,21},{6,22},{7,23},{8,136... | collective-permute-start | bytes 491528 | tf_op jit(solution)/shard_map/ppermute | solution.py:69
  27.4 2.7 %collective-permute-done.5.refs_2_ = f32[32,1280]{1,0:T(8,128)S(1)} collective-permute-done((f32[32,1280]{1,0:T(8,128)S(1)}, f32[32,1280]{1,0:T(8,128)S(1)}, u32[]{:S(2)}, u32[]{:S(2)}) %collective-permute-start.5) | collective-permute-done | bytes 163872 | tf_op jit(solution)/shard_map/ppermute | solution.py:69
  30.2 3.4 %collective-permute-start.7 = (f32[4,32,1280]{2,1,0:T(8,128)S(1)}, f32[4,32,1280]{2,1,0:T(8,128)S(1)}, u32[]{:S(2)}, u32[]{:S(2)}) collective-permute-start(f32[4,32,1280]{2,1,0:T(8,128)S(1)} %join.4.refs_0_), channel_id=1, source_target_pairs={{0,8},{1,9},{2,10},{3,11},{4,68},{5,69},{6,70},{7,71},{8,16},{9,17... | collective-permute-start | bytes 1966088 | tf_op jit(solution)/shard_map/ppermute | solution.py:69
  34.0 4.4 %collective-permute-start.9 = (f32[4,32,1280]{2,1,0:T(8,128)S(1)}, f32[4,32,1280]{2,1,0:T(8,128)S(1)}, u32[]{:S(2)}, u32[]{:S(2)}) collective-permute-start(f32[4,32,1280]{2,1,0:T(8,128)S(1)} %join.4.refs_0_), channel_id=1, source_target_pairs={{0,32},{1,33},{2,34},{3,35},{4,39},{5,36},{6,37},{7,38},{8,40},{9,... | collective-permute-start | bytes 1966088 | tf_op jit(solution)/shard_map/ppermute | solution.py:69
  39.1 1.6 %copy-done = f32[1,1024,512]{2,1,0:T(8,128)S(1)} copy-done((f32[1,1024,512]{2,1,0:T(8,128)S(1)}, f32[1,1024,512]{2,1,0:T(8,128)}, u32[]{:S(2)}) %copy-start) | copy-done | bytes 2097176
  41.9 1.9 %update.1 = (bf16[512,1024]{1,0:T(8,128)(2,1)S(1)}, bf16[512,1024]{1,0:T(8,128)(2,1)S(1)}, f32[1,512]{1,0:T(1,128)S(1)}) custom-call(s32[1]{0:T(128)S(6)} %copy.8.width_ref, f32[1,512,512]{2,1,0:T(8,128)S(1)} %copy-done.1, f32[1,1024,512]{2,1,0:T(8,128)S(1)} %copy-done), custom_call_target="tpu_custom_call" | custom-call | flops 1610612736 | bytes 5242880 | tf_op jit(solution)/shard_map/update/pallas_call | solution.py:104
  43.8 2.9 %collective-permute-done.9.quad.refs_3_ = f32[4,32,1280]{2,1,0:T(8,128)S(1)} collective-permute-done((f32[4,32,1280]{2,1,0:T(8,128)S(1)}, f32[4,32,1280]{2,1,0:T(8,128)S(1)}, u32[]{:S(2)}, u32[]{:S(2)}) %collective-permute-start.9) | collective-permute-done | bytes 655392 | tf_op jit(solution)/shard_map/ppermute | solution.py:69
  46.8 1.5 %collective-permute-start.10 = (f32[4,32,1280]{2,1,0:T(8,128)S(1)}, f32[4,32,1280]{2,1,0:T(8,128)S(1)}, u32[]{:S(2)}, u32[]{:S(2)}) collective-permute-start(f32[4,32,1280]{2,1,0:T(8,128)S(1)} %get-tuple-element.59), channel_id=1, source_target_pairs={{0,8},{1,9},{2,10},{3,11},{4,68},{5,69},{6,70},{7,71},{8,16},{9,17... | collective-permute-start | bytes 1966088 | tf_op jit(solution)/shard_map/ppermute | solution.py:69
  49.6 2.7 %collective-permute-start.12 = (f32[4,32,1280]{2,1,0:T(8,128)S(1)}, f32[4,32,1280]{2,1,0:T(8,128)S(1)}, u32[]{:S(2)}, u32[]{:S(2)}) collective-permute-start(f32[4,32,1280]{2,1,0:T(8,128)S(1)} %get-tuple-element.61), channel_id=1, source_target_pairs={{0,32},{1,33},{2,34},{3,35},{4,39},{5,36},{6,37},{7,38},{8,40},{9,... | collective-permute-start | bytes 1966088 | tf_op jit(solution)/shard_map/ppermute | solution.py:69
  52.4 2.0 %collective-permute-start.13 = (f32[16,32,1280]{2,1,0:T(8,128)S(1)}, f32[16,32,1280]{2,1,0:T(8,128)S(1)}, u32[]{:S(2)}, u32[]{:S(2)}) collective-permute-start(f32[16,32,1280]{2,1,0:T(8,128)S(1)} %join.5.near), channel_id=1, source_target_pairs={{0,4},{1,5},{2,6},{3,7},{4,0},{5,1},{6,2},{7,3},{8,12},{9,13},{10,... | collective-permute-start | bytes 7864328 | tf_op jit(solution)/shard_map/ppermute | solution.py:69
  54.5 3.4 %collective-permute-done.10.ahead.refs_0_ = f32[4,32,1280]{2,1,0:T(8,128)S(1)} collective-permute-done((f32[4,32,1280]{2,1,0:T(8,128)S(1)}, f32[4,32,1280]{2,1,0:T(8,128)S(1)}, u32[]{:S(2)}, u32[]{:S(2)}) %collective-permute-start.10) | collective-permute-done | bytes 655392 | tf_op jit(solution)/shard_map/ppermute | solution.py:69
  58.2 2.4 %collective-permute-done.12.refs_2_ = f32[4,32,1280]{2,1,0:T(8,128)S(1)} collective-permute-done((f32[4,32,1280]{2,1,0:T(8,128)S(1)}, f32[4,32,1280]{2,1,0:T(8,128)S(1)}, u32[]{:S(2)}, u32[]{:S(2)}) %collective-permute-start.12) | collective-permute-done | bytes 655392 | tf_op jit(solution)/shard_map/ppermute | solution.py:69
  60.7 3.1 %collective-permute-start.14 = (f32[12,32,1280]{2,1,0:T(8,128)S(1)}, f32[12,32,1280]{2,1,0:T(8,128)S(1)}, u32[]{:S(2)}, u32[]{:S(2)}) collective-permute-start(f32[12,32,1280]{2,1,0:T(8,128)S(1)} %join.6.side), channel_id=1, source_target_pairs={{0,4},{1,5},{2,6},{3,7},{4,0},{5,1},{6,2},{7,3},{8,12},{9,13},{10,... | collective-permute-start | bytes 5898248 | tf_op jit(solution)/shard_map/ppermute | solution.py:69
  63.8 1.4 %collective-permute-start.15 = (f32[2,32,1280]{2,1,0:T(8,128)S(1)}, f32[2,32,1280]{2,1,0:T(8,128)S(1)}, u32[]{:S(2)}, u32[]{:S(2)}) collective-permute-start(f32[2,32,1280]{2,1,0:T(8,128)S(1)} %get-tuple-element.67), channel_id=1, source_target_pairs={{0,8},{1,9},{2,10},{3,11},{4,68},{5,69},{6,70},{7,71},{8,16},{9,17... | collective-permute-start | bytes 983048 | tf_op jit(solution)/shard_map/ppermute | solution.py:69
  65.2 1.3 %collective-permute-start.16 = (f32[2,32,1280]{2,1,0:T(8,128)S(1)}, f32[2,32,1280]{2,1,0:T(8,128)S(1)}, u32[]{:S(2)}, u32[]{:S(2)}) collective-permute-start(f32[2,32,1280]{2,1,0:T(8,128)S(1)} %get-tuple-element.68), channel_id=1, source_target_pairs={{0,24},{1,25},{2,26},{3,27},{4,196},{5,197},{6,198},{7,199},{8,0},... | collective-permute-start | bytes 983048 | tf_op jit(solution)/shard_map/ppermute | solution.py:69
  66.5 4.8 %collective-permute-done.15.refs_0_ = f32[2,32,1280]{2,1,0:T(8,128)S(1)} collective-permute-done((f32[2,32,1280]{2,1,0:T(8,128)S(1)}, f32[2,32,1280]{2,1,0:T(8,128)S(1)}, u32[]{:S(2)}, u32[]{:S(2)}) %collective-permute-start.15) | collective-permute-done | bytes 327712 | tf_op jit(solution)/shard_map/ppermute | solution.py:69
  72.5 4.1 %lay.1 = (bf16[1664,2048]{1,0:T(8,128)(2,1)S(1)}, bf16[1664,2048]{1,0:T(8,128)(2,1)S(1)}) custom-call(s32[5]{0:T(128)S(1)} %stack.23.where_ref, s32[1,8]{1,0:T(1,128)S(1)} %copy-done.2, f32[16,32,1280]{2,1,0:T(8,128)S(1)} %join.5.near, f32[12,32,1280]{2,1,0:T(8,128)S(1)} %join.6.side, f32[16,32,1280]{2,1,0:T(8,128)S(1)} %collective-permute-done.13.other_near, ...), custom_call_target="tpu_custom_call" | custom-call | flops 10000000000 | bytes 10485760 | tf_op jit(solution)/shard_map/lay/pallas_call | solution.py:312
  76.6 13.9 %final.1 = (f32[1,1024,512]{2,1,0:T(8,128)}, f32[1,512]{1,0:T(1,128)}, f32[32,512]{1,0:T(8,128)}) custom-call(s32[5]{0:T(128)S(1)} %stack.23.where_ref, s32[1,8]{1,0:T(1,128)S(1)} %copy-done.2, bf16[512,1024]{1,0:T(8,128)(2,1)S(1)} %get-tuple-element.45.high_ref, bf16[512,1024]{1,0:T(8,128)(2,1)S(1)} %get-tuple-element.46.low_ref, ...), custom_call_target="tpu_custom_call" | custom-call | flops 10000000000 | bytes 10485760 | tf_op jit(solution)/shard_map/final/pallas_call | solution.py:448
  (30 shorter events, 8.2 us)
Async XLA Ops:
  0.6 1.5 %collective-permute-start = (f32[32,512]{1,0:T(8,128)}, f32[32,512]{1,0:T(8,128)S(1)}, u32[]{:S(2)}, u32[]{:S(2)}) collective-permute-start(f32[32,512]{1,0:T(8,128)} %bitcast.8), channel_id=1, source_target_pairs={{0,0},{1,193},{2,194},{3,3},{4,4},{5,197},{6,198},{7,7},{8,8},{9,2... | collective-permute-start | bytes 196616 | tf_op jit(solution)/shard_map/ppermute | solution.py:69
  3.0 16.5 %collective-permute-start.1 = (f32[32,512]{1,0:T(8,128)S(1)}, f32[32,512]{1,0:T(8,128)S(1)}, u32[]{:S(2)}, u32[]{:S(2)}) collective-permute-start(f32[32,512]{1,0:T(8,128)S(1)} %broadcast_select_fusion.refs_0_), channel_id=1, source_target_pairs={{0,1},{1,2},{2,3},{3,0},{4,5},{5,6},{6,7},{7,4},{8,9},{9,10},{10,1... | collective-permute-start | bytes 196616 | tf_op jit(solution)/shard_map/ppermute | solution.py:69
  11.9 7.6 %collective-permute-start.2 = (f32[32,512]{1,0:T(8,128)S(1)}, f32[32,512]{1,0:T(8,128)S(1)}, u32[]{:S(2)}, u32[]{:S(2)}) collective-permute-start(f32[32,512]{1,0:T(8,128)S(1)} %broadcast_select_fusion.refs_0_), channel_id=1, source_target_pairs={{0,2},{1,3},{2,0},{3,1},{4,6},{5,7},{6,4},{7,5},{8,10},{9,11},{10,... | collective-permute-start | bytes 196616 | tf_op jit(solution)/shard_map/ppermute | solution.py:69
  15.9 5.4 %collective-permute-start.3 = (f32[32,512]{1,0:T(8,128)S(1)}, f32[32,512]{1,0:T(8,128)S(1)}, u32[]{:S(2)}, u32[]{:S(2)}) collective-permute-start(f32[32,512]{1,0:T(8,128)S(1)} %broadcast_select_fusion.refs_0_), channel_id=1, source_target_pairs={{0,3},{1,0},{2,1},{3,2},{4,7},{5,4},{6,5},{7,6},{8,11},{9,8},{10,9... | collective-permute-start | bytes 196616 | tf_op jit(solution)/shard_map/ppermute | solution.py:69
  22.0 5.5 %collective-permute-start.4 = (f32[32,1280]{1,0:T(8,128)S(1)}, f32[32,1280]{1,0:T(8,128)S(1)}, u32[]{:S(2)}, u32[]{:S(2)}) collective-permute-start(f32[32,1280]{1,0:T(8,128)S(1)} %line.1.refs_0_), channel_id=1, source_target_pairs={{0,64},{1,65},{2,66},{3,67},{4,12},{5,13},{6,14},{7,15},{8,72},{9,... | collective-permute-start | bytes 491528 | tf_op jit(solution)/shard_map/ppermute | solution.py:69
  23.3 6.9 %collective-permute-start.5 = (f32[32,1280]{1,0:T(8,128)S(1)}, f32[32,1280]{1,0:T(8,128)S(1)}, u32[]{:S(2)}, u32[]{:S(2)}) collective-permute-start(f32[32,1280]{1,0:T(8,128)S(1)} %line.1.refs_0_), channel_id=1, source_target_pairs={{0,128},{1,129},{2,130},{3,131},{4,20},{5,21},{6,22},{7,23},{8,136... | collective-permute-start | bytes 491528 | tf_op jit(solution)/shard_map/ppermute | solution.py:69
  25.7 4.5 %collective-permute-start.6 = (f32[32,1280]{1,0:T(8,128)S(1)}, f32[32,1280]{1,0:T(8,128)S(1)}, u32[]{:S(2)}, u32[]{:S(2)}) collective-permute-start(f32[32,1280]{1,0:T(8,128)S(1)} %line.1.refs_0_), channel_id=1, source_target_pairs={{0,192},{1,193},{2,194},{3,195},{4,28},{5,29},{6,30},{7,31},{8,200... | collective-permute-start | bytes 491528 | tf_op jit(solution)/shard_map/ppermute | solution.py:69
  30.2 13.6 %collective-permute-start.7 = (f32[4,32,1280]{2,1,0:T(8,128)S(1)}, f32[4,32,1280]{2,1,0:T(8,128)S(1)}, u32[]{:S(2)}, u32[]{:S(2)}) collective-permute-start(f32[4,32,1280]{2,1,0:T(8,128)S(1)} %join.4.refs_0_), channel_id=1, source_target_pairs={{0,8},{1,9},{2,10},{3,11},{4,68},{5,69},{6,70},{7,71},{8,16},{9,17... | collective-permute-start | bytes 1966088 | tf_op jit(solution)/shard_map/ppermute | solution.py:69
  33.7 10.2 %collective-permute-start.8 = (f32[4,32,1280]{2,1,0:T(8,128)S(1)}, f32[4,32,1280]{2,1,0:T(8,128)S(1)}, u32[]{:S(2)}, u32[]{:S(2)}) collective-permute-start(f32[4,32,1280]{2,1,0:T(8,128)S(1)} %join.4.refs_0_), channel_id=1, source_target_pairs={{0,24},{1,25},{2,26},{3,27},{4,196},{5,197},{6,198},{7,199},{8,0},... | collective-permute-start | bytes 1966088 | tf_op jit(solution)/shard_map/ppermute | solution.py:69
  34.0 12.7 %collective-permute-start.9 = (f32[4,32,1280]{2,1,0:T(8,128)S(1)}, f32[4,32,1280]{2,1,0:T(8,128)S(1)}, u32[]{:S(2)}, u32[]{:S(2)}) collective-permute-start(f32[4,32,1280]{2,1,0:T(8,128)S(1)} %join.4.refs_0_), channel_id=1, source_target_pairs={{0,32},{1,33},{2,34},{3,35},{4,39},{5,36},{6,37},{7,38},{8,40},{9,... | collective-permute-start | bytes 1966088 | tf_op jit(solution)/shard_map/ppermute | solution.py:69
  39.1 1.6 %copy-start = (f32[1,1024,512]{2,1,0:T(8,128)S(1)}, f32[1,1024,512]{2,1,0:T(8,128)}, u32[]{:S(2)}) copy-start(f32[1,1024,512]{2,1,0:T(8,128)} %panel_ref) | copy-start | bytes 6291460
  40.7 1.2 %copy-start.1 = (f32[1,512,512]{2,1,0:T(8,128)S(1)}, f32[1,512,512]{2,1,0:T(8,128)}, u32[]{:S(2)}) copy-start(f32[1,512,512]{2,1,0:T(8,128)} %inverse_ref) | copy-start | bytes 3145732
  46.8 11.0 %collective-permute-start.10 = (f32[4,32,1280]{2,1,0:T(8,128)S(1)}, f32[4,32,1280]{2,1,0:T(8,128)S(1)}, u32[]{:S(2)}, u32[]{:S(2)}) collective-permute-start(f32[4,32,1280]{2,1,0:T(8,128)S(1)} %get-tuple-element.59), channel_id=1, source_target_pairs={{0,8},{1,9},{2,10},{3,11},{4,68},{5,69},{6,70},{7,71},{8,16},{9,17... | collective-permute-start | bytes 1966088 | tf_op jit(solution)/shard_map/ppermute | solution.py:69
  48.4 9.7 %collective-permute-start.11 = (f32[4,32,1280]{2,1,0:T(8,128)S(1)}, f32[4,32,1280]{2,1,0:T(8,128)S(1)}, u32[]{:S(2)}, u32[]{:S(2)}) collective-permute-start(f32[4,32,1280]{2,1,0:T(8,128)S(1)} %get-tuple-element.60), channel_id=1, source_target_pairs={{0,24},{1,25},{2,26},{3,27},{4,196},{5,197},{6,198},{7,199},{8,0},... | collective-permute-start | bytes 1966088 | tf_op jit(solution)/shard_map/ppermute | solution.py:69
  49.6 10.9 %collective-permute-start.12 = (f32[4,32,1280]{2,1,0:T(8,128)S(1)}, f32[4,32,1280]{2,1,0:T(8,128)S(1)}, u32[]{:S(2)}, u32[]{:S(2)}) collective-permute-start(f32[4,32,1280]{2,1,0:T(8,128)S(1)} %get-tuple-element.61), channel_id=1, source_target_pairs={{0,32},{1,33},{2,34},{3,35},{4,39},{5,36},{6,37},{7,38},{8,40},{9,... | collective-permute-start | bytes 1966088 | tf_op jit(solution)/shard_map/ppermute | solution.py:69
  52.4 20.1 %collective-permute-start.13 = (f32[16,32,1280]{2,1,0:T(8,128)S(1)}, f32[16,32,1280]{2,1,0:T(8,128)S(1)}, u32[]{:S(2)}, u32[]{:S(2)}) collective-permute-start(f32[16,32,1280]{2,1,0:T(8,128)S(1)} %join.5.near), channel_id=1, source_target_pairs={{0,4},{1,5},{2,6},{3,7},{4,0},{5,1},{6,2},{7,3},{8,12},{9,13},{10,... | collective-permute-start | bytes 7864328 | tf_op jit(solution)/shard_map/ppermute | solution.py:69
  60.5 12.0 %copy-start.2 = (s32[1,8]{1,0:T(1,128)S(1)}, s32[1,8]{1,0:T(1,128)}, u32[]{:S(2)}) copy-start(s32[1,8]{1,0:T(1,128)} %structure_ref.3) | copy-start | bytes 100
  60.7 10.8 %collective-permute-start.14 = (f32[12,32,1280]{2,1,0:T(8,128)S(1)}, f32[12,32,1280]{2,1,0:T(8,128)S(1)}, u32[]{:S(2)}, u32[]{:S(2)}) collective-permute-start(f32[12,32,1280]{2,1,0:T(8,128)S(1)} %join.6.side), channel_id=1, source_target_pairs={{0,4},{1,5},{2,6},{3,7},{4,0},{5,1},{6,2},{7,3},{8,12},{9,13},{10,... | collective-permute-start | bytes 5898248 | tf_op jit(solution)/shard_map/ppermute | solution.py:69
  63.8 7.4 %collective-permute-start.15 = (f32[2,32,1280]{2,1,0:T(8,128)S(1)}, f32[2,32,1280]{2,1,0:T(8,128)S(1)}, u32[]{:S(2)}, u32[]{:S(2)}) collective-permute-start(f32[2,32,1280]{2,1,0:T(8,128)S(1)} %get-tuple-element.67), channel_id=1, source_target_pairs={{0,8},{1,9},{2,10},{3,11},{4,68},{5,69},{6,70},{7,71},{8,16},{9,17... | collective-permute-start | bytes 983048 | tf_op jit(solution)/shard_map/ppermute | solution.py:69
  65.2 6.2 %collective-permute-start.16 = (f32[2,32,1280]{2,1,0:T(8,128)S(1)}, f32[2,32,1280]{2,1,0:T(8,128)S(1)}, u32[]{:S(2)}, u32[]{:S(2)}) collective-permute-start(f32[2,32,1280]{2,1,0:T(8,128)S(1)} %get-tuple-element.68), channel_id=1, source_target_pairs={{0,24},{1,25},{2,26},{3,27},{4,196},{5,197},{6,198},{7,199},{8,0},... | collective-permute-start | bytes 983048 | tf_op jit(solution)/shard_map/ppermute | solution.py:69
  71.5 5.1 %collective-permute-start.17 = (f32[4,32,1280]{2,1,0:T(8,128)S(1)}, f32[4,32,1280]{2,1,0:T(8,128)S(1)}, u32[]{:S(2)}, u32[]{:S(2)}) collective-permute-start(f32[4,32,1280]{2,1,0:T(8,128)S(1)} %join.7.far), channel_id=1, source_target_pairs={{0,4},{1,5},{2,6},{3,7},{4,0},{5,1},{6,2},{7,3},{8,12},{9,13},{10,... | collective-permute-start | bytes 1966088 | tf_op jit(solution)/shard_map/ppermute | solution.py:69
